TPU v7x, 256 devices: a whole 4x4x8 slice. The times are simulated.
256 devices in a mesh: row: 8 (over z_lo, core), col: 32 (over x, z_hi, y).
Axes of the slice: x: 4, y: 4, z: 8 (z_hi: 2, z_lo: 4; z = z_hi * 4 + z_lo), core: 2. Of those that a mesh axis runs over, the one named last changes fastest.
Arguments:
- pair_rep: bfloat16 [1024, 1024, 128], P('row', 'col'), may hold values from -6 to 6
- residue_mask: int32 [1024], replicated, may hold values 0 or 1
- in_gain: float32 [128], replicated, may hold values from 0.25 to 1.75
- in_bias: float32 [128], replicated, may hold values from -3 to 3
- in_weights: bfloat16 [4, 128, 128], replicated, may hold values from -3 to 3
- gate_weight: bfloat16 [128, 128], replicated, may hold values from -0.5 to 0.5
- out_gain: float32 [128], replicated, may hold values from 0.25 to 1.75
- out_bias: float32 [128], replicated, may hold values from -3 to 3
- out_weight: bfloat16 [128, 128], replicated, may hold values from -0.5 to 0.5
Outputs:
- update: bfloat16 [1024, 1024, 128], P('row', 'col')
All inputs are finite; a program needn't handle non-finite values.
Results may differ from a plain program's by a relative error of at most 0.0057.
Values may be sent and summed in bfloat16 or wider, within the bound.
No kernel may reach another device: no remote copies, remote signals or barrier semaphores. Data moves between devices by JAX's collectives and lax.ppermute only.
A program may use at most 128 MiB of HBM per device.

v0:
```python
import jax
import jax.numpy as jnp
from jax import lax
from jax.sharding import PartitionSpec as P


def layer_norm(values, gain_vec, offset, axis_dim):
    average = jnp.mean(values, axis=axis_dim, keepdims=True)
    centred = values - average
    spread = jnp.mean(centred * centred, axis=axis_dim, keepdims=True)
    return centred * lax.rsqrt(spread + 1e-05) * gain_vec + offset


def products(left_share, right_piece):
    return jnp.einsum(
        "hik,hjk->hij", left_share, right_piece, preferred_element_type=jnp.float32
    ).astype(jnp.bfloat16)


def local(
    pair_rep,
    residue_mask,
    in_gain,
    in_bias,
    in_weights,
    gate_weight,
    out_gain,
    out_bias,
    out_weight,
):
    rows_here, cols_here, channels = pair_rep.shape
    hidden = in_weights.shape[2]
    row_mask = lax.dynamic_slice_in_dim(
        residue_mask, lax.axis_index("row") * rows_here, rows_here, 0
    ).astype(jnp.float32)
    col_mask = lax.dynamic_slice_in_dim(
        residue_mask, lax.axis_index("col") * cols_here, cols_here, 0
    ).astype(jnp.float32)
    normed_in = layer_norm(pair_rep.astype(jnp.float32), in_gain, in_bias, 2).astype(jnp.bfloat16)
    flattened = normed_in.reshape(rows_here * cols_here, channels)
    joined = jnp.concatenate(
        [in_weights[0], in_weights[1], in_weights[2], in_weights[3], gate_weight], axis=1
    )
    projected = jnp.dot(flattened, joined, preferred_element_type=jnp.float32)
    projected = projected.reshape(rows_here, cols_here, 4 * hidden + channels)
    pair_mask = (row_mask[:, None] * col_mask[None, :])[:, :, None]
    left_tile = (
        jax.nn.sigmoid(projected[:, :, :hidden]) * projected[:, :, hidden : 2 * hidden] * pair_mask
    )
    right_tile = (
        jax.nn.sigmoid(projected[:, :, 2 * hidden : 3 * hidden])
        * projected[:, :, 3 * hidden : 4 * hidden]
        * pair_mask
    )
    left_tile = left_tile.astype(jnp.bfloat16).transpose(2, 0, 1)
    right_tile = right_tile.astype(jnp.bfloat16).transpose(2, 0, 1)
    gate_term = jax.nn.sigmoid(projected[:, :, 4 * hidden :])
    whole_right = lax.all_gather(right_tile, "row", axis=1, tiled=True)
    left_share = lax.all_to_all(left_tile, "col", split_axis=0, concat_axis=2, tiled=True)
    triangle = products(
        left_share, lax.all_to_all(whole_right, "col", split_axis=0, concat_axis=2, tiled=True)
    )
    normed_out = layer_norm(
        lax.all_to_all(triangle, "col", split_axis=2, concat_axis=0, tiled=True).astype(
            jnp.float32
        ),
        out_gain[:, None, None],
        out_bias[:, None, None],
        0,
    )
    normed_out = normed_out.astype(jnp.bfloat16)
    out_proj = jnp.einsum("hij,hc->ijc", normed_out, out_weight, preferred_element_type=jnp.float32)
    return (gate_term * out_proj).astype(jnp.bfloat16)


def solution(mesh):
    placed = (P("row", "col", None), P(), P(), P(), P(), P(), P(), P(), P())
    return jax.shard_map(
        local, mesh=mesh, in_specs=placed, out_specs=P("row", "col", None), check_vma=False
    )
```

profile of v0, /device:TPU:8, one launch (start us, length us, event | category | flops | bytes accessed | tf_op | source)
XLA Modules:
  0.0 429.6 jit_solution(13143589910275541196)
XLA Ops:
  6.5 0.0 copy-start
  6.5 0.0 copy-start.2
  6.5 0.0 copy-start.8
  6.6 0.0 all-gather.2.cloned.1.call-start
  6.6 0.8 dynamic-slice_convert_fusion
  7.5 0.8 dynamic-slice_convert_fusion.1
  8.2 1.8 convert_reduce_fusion
  10.1 0.1 copy.62
  10.1 0.1 copy.63
  10.2 2.3 fusion.2
  12.6 0.1 copy.64
  12.7 0.1 copy.65
  12.8 0.0 copy-done.3
  12.8 0.1 broadcast_multiply_fusion
  12.9 0.0 copy-done.4
  12.9 0.0 copy-done.2
  12.9 0.0 copy-done.7
  13.0 0.0 copy-done.8
  13.0 1.5 fusion.5
  14.5 1.5 fusion.27
  16.0 0.0 copy-start.1
  16.0 2.6 fusion.30
  18.6 1.6 copy-done.1
  20.2 0.0 all-gather.2.cloned.1.call-update
  20.3 1.7 copy.67
  22.0 14.2 %all-to-all-start = ((bf16[128,128,32]{1,2,0:T(8,128)(2,1)}), bf16[128,128,32]{1,2,0:T(8,128)(2,1)S(1)}, u32[]{:S(2)}, u32[]{:S(2)}) async-start(bf16[128,128,32]{1,2,0:T(8,128)(2,1)} %copy.67), calls=%async_computation | async-start | bytes 2097152 | tf_op jit(solution)/shard_map/all_to_all | solution.py:59
  36.2 103.8 %all-gather.2.cloned.1.call-done = bf16[128,1024,32]{0,1,2:T(8,128)(2,1)} async-done(((bf16[128,128,32]{0,1,2:T(8,128)(2,1)}), bf16[128,1024,32]{0,1,2:T(8,128)(2,1)}) %all-gather.2.cloned.1.call-update) | async-done | bytes 8388624 | tf_op jit(solution)/shard_map/all_gather | solution.py:58
  139.9 12.4 %copy.69 = bf16[128,1024,32]{1,2,0:T(8,128)(2,1)} copy(bf16[128,1024,32]{0,1,2:T(8,128)(2,1)} %all-gather.2.cloned.1.call-done) | data formatting | bytes 16777216 | tf_op jit(solution)/shard_map/all_gather | solution.py:58
  152.3 0.0 all-to-all-done
  152.3 9.8 %all-to-all-start.1 = ((bf16[128,1024,32]{1,2,0:T(8,128)(2,1)}), bf16[128,1024,32]{1,2,0:T(8,128)(2,1)}, u32[]{:S(2)}, u32[]{:S(2)}) async-start(bf16[128,1024,32]{1,2,0:T(8,128)(2,1)} %copy.69), calls=%async_computation.1 | async-start | bytes 16777216 | tf_op jit(solution)/shard_map/all_to_all | solution.py:61
  162.1 0.1 copy.68
  162.2 201.8 %all-to-all-done.1 = bf16[128,1024,32]{1,2,0:T(8,128)(2,1)} async-done(((bf16[128,1024,32]{1,2,0:T(8,128)(2,1)}), bf16[128,1024,32]{1,2,0:T(8,128)(2,1)}, u32[]{:S(2)}, u32[]{:S(2)}) %all-to-all-start.1) | async-done | bytes 8388640 | tf_op jit(solution)/shard_map/all_to_all | solution.py:61
  364.0 8.6 %copy.70 = bf16[4,1024,32,32]{1,3,2,0:T(8,128)(2,1)} copy(bf16[4,1024,32,32]{1,3,0,2:T(8,128)(2,1)} %bitcast.11) | data formatting | bytes 16777216 | tf_op jit(solution)/shard_map/all_to_all | solution.py:61
  372.6 4.7 %convolution_convert_fusion = bf16[4,128,1024]{2,1,0:T(8,128)(2,1)S(1)} fusion(bf16[4,128,1024]{1,2,0:T(8,128)(2,1)S(1)} %bitcast.50, bf16[4,1024,1024]{1,2,0:T(8,128)(2,1)} %bitcast.47), kind=kOutput, calls=%fused_computation.35 | convolution fusion | flops 1074266112 | bytes 10485760 | tf_op jit(solution)/shard_map/hik,hjk->hij/dot_general | solution.py:15
  377.3 0.8 copy.73
  378.1 38.6 %all_to_all.45 = bf16[4,128,1024]{1,0,2:T(4,128)(2,1)S(1)} all-to-all(bf16[4,128,1024]{1,0,2:T(4,128)(2,1)S(1)} %copy.73), channel_id=1, replica_groups=mesh['row'=8,'col'=32] {'col'}, dimensions={2} | all-to-all | bytes 2097152 | tf_op jit(solution)/shard_map/all_to_all | solution.py:64
  416.7 0.3 fusion.33
  417.0 0.2 fusion.25
  417.2 0.3 multiply_reduce_fusion
  417.5 0.0 copy-start.5
  417.5 0.0 copy-start.6
  417.5 0.2 copy.75
  417.8 0.4 copy-done.5
  418.2 0.0 copy-done.6
  418.2 0.4 fusion.23
  418.6 0.0 copy-done
  418.6 2.5 fusion.24
  421.1 1.6 copy.77
  (12 shorter events, 0.1 us)
Async XLA Ops:
  6.5 412.1 %copy-start = (bf16[128,128]{1,0:T(8,128)(2,1)S(1)}, bf16[128,128]{1,0:T(8,128)(2,1)}, u32[]{:S(2)}) copy-start(bf16[128,128]{1,0:T(8,128)(2,1)} %param.17) | copy-start | bytes 98308
  6.5 6.4 %copy-start.2 = (bf16[128,32,128]{2,1,0:T(8,128)(2,1)S(1)}, bf16[128,32,128]{2,1,0:T(8,128)(2,1)}, u32[]{:S(2)}) copy-start(bf16[128,32,128]{2,1,0:T(8,128)(2,1)} %param.9) | copy-start | bytes 3145732
  6.5 6.2 %copy-start.3 = (bf16[4,128,128]{2,1,0:T(8,128)(2,1)S(1)}, bf16[4,128,128]{2,1,0:T(8,128)(2,1)}, u32[]{:S(2)}) copy-start(bf16[4,128,128]{2,1,0:T(8,128)(2,1)} %param.13) | copy-start | bytes 393220
  6.5 6.4 %copy-start.4 = (bf16[128,128]{1,0:T(8,128)(2,1)S(1)}, bf16[128,128]{1,0:T(8,128)(2,1)}, u32[]{:S(2)}) copy-start(bf16[128,128]{1,0:T(8,128)(2,1)} %param.14) | copy-start | bytes 98308
  6.5 6.4 %copy-start.7 = (f32[128]{0:T(128)S(1)}, f32[128]{0:T(128)}, u32[]{:S(2)}) copy-start(f32[128]{0:T(128)} %param.12) | copy-start | bytes 1540
  6.5 6.4 %copy-start.8 = (f32[128]{0:T(128)S(1)}, f32[128]{0:T(128)}, u32[]{:S(2)}) copy-start(f32[128]{0:T(128)} %param.11) | copy-start | bytes 1540
  6.6 133.4 %all-gather.2.cloned.1.call-start = ((), (), s32[]{:S(2)}) async-start(), calls=%async_computation.3 | async-start | bytes 9437184 | tf_op jit(solution)/shard_map/all_gather | solution.py:58
  16.0 4.2 copy-start.1
  22.0 130.3 %all-to-all-start = ((bf16[128,128,32]{1,2,0:T(8,128)(2,1)}), bf16[128,128,32]{1,2,0:T(8,128)(2,1)S(1)}, u32[]{:S(2)}, u32[]{:S(2)}) async-start(bf16[128,128,32]{1,2,0:T(8,128)(2,1)} %copy.67), calls=%async_computation | async-start | bytes 2097152 | tf_op jit(solution)/shard_map/all_to_all | solution.py:59
  152.3 211.7 %all-to-all-start.1 = ((bf16[128,1024,32]{1,2,0:T(8,128)(2,1)}), bf16[128,1024,32]{1,2,0:T(8,128)(2,1)}, u32[]{:S(2)}, u32[]{:S(2)}) async-start(bf16[128,1024,32]{1,2,0:T(8,128)(2,1)} %copy.69), calls=%async_computation.1 | async-start | bytes 16777216 | tf_op jit(solution)/shard_map/all_to_all | solution.py:61
  417.5 0.7 copy-start.5
  417.5 0.7 copy-start.6
Sparse Core Ops, SparseCore 0:
  20.4 119.5 all-gather.1
where the time goes:
time: 430 us
  waiting for transfers between devices  306 us (71%)
  blocking collectives  38.6 us (9%)
  local copies, waits for them, and re-layouts  27.8 us (6%)
  starting transfers between devices  24 us (6%)
  between operations  13.6 us (3%)
  other arithmetic  11.2 us (3%)
  matrix products  8.74 us (2%)
    all_to_all x1, waiting for transfers between devices, local(): lax.all_to_all(whole_right, 'col', split_axis=0, concat_axis=2, tiled=True)  202 us
    all_gather x1, waiting for transfers between devices, local(): whole_right = lax.all_gather(right_tile, 'row', axis=1, tiled=True)  104 us
    all_to_all x1, blocking collectives, local(): lax.all_to_all(triangle, 'col', split_axis=2, concat_axis=0, tiled=True)  38.6 us
    all_to_all x1, starting transfers between devices, local(): lax.all_to_all(left_tile, 'col', split_axis=0, concat_axis=2, tiled=True)  14.2 us
    all_gather x1, local copies, waits for them, and re-layouts, local(): whole_right = lax.all_gather(right_tile, 'row', axis=1, tiled=True)  12.4 us
    all_to_all x1, starting transfers between devices, local(): lax.all_to_all(whole_right, 'col', split_axis=0, concat_axis=2, tiled=True)  9.81 us
  transfers between devices with their start and end apart: 3, of which 2 were waited for; matrix products, arithmetic and copies ran while one was open for 3% of the time, Pallas kernels for 0%

commit v1 on v0

v1 whole, which is shorter than its diff:
```python
import jax
import jax.numpy as jnp
from jax import lax
from jax.sharding import Mesh
from jax.sharding import PartitionSpec as P

CHIPS = ("zl", "x", "zh", "y")


def layer_norm(values, gain_vec, offset, axis_dim):
    average = jnp.mean(values, axis=axis_dim, keepdims=True)
    centred = values - average
    spread = jnp.mean(centred * centred, axis=axis_dim, keepdims=True)
    return centred * lax.rsqrt(spread + 1e-05) * gain_vec + offset


def swap(chunks):
    return lax.all_to_all(chunks, CHIPS, split_axis=0, concat_axis=0, tiled=True)


def local(
    pair_rep,
    residue_mask,
    in_gain,
    in_bias,
    in_weights,
    gate_weight,
    out_gain,
    out_bias,
    out_weight,
):
    rows_here, cols_here, channels = pair_rep.shape
    hidden = in_weights.shape[2]
    row_mask = lax.dynamic_slice_in_dim(
        residue_mask, lax.axis_index(("zl", "core")) * rows_here, rows_here, 0
    ).astype(jnp.float32)
    col_mask = lax.dynamic_slice_in_dim(
        residue_mask, lax.axis_index(("x", "zh", "y")) * cols_here, cols_here, 0
    ).astype(jnp.float32)
    normed_in = layer_norm(pair_rep.astype(jnp.float32), in_gain, in_bias, 2).astype(jnp.bfloat16)
    flattened = normed_in.reshape(rows_here * cols_here, channels)
    joined = jnp.concatenate(
        [in_weights[0], in_weights[1], in_weights[2], in_weights[3], gate_weight], axis=1
    )
    projected = jnp.dot(flattened, joined, preferred_element_type=jnp.float32)
    projected = projected.reshape(rows_here, cols_here, 4 * hidden + channels)
    pair_mask = (row_mask[:, None] * col_mask[None, :])[:, :, None]
    left_tile = (
        jax.nn.sigmoid(projected[:, :, :hidden]) * projected[:, :, hidden : 2 * hidden] * pair_mask
    )
    right_tile = (
        jax.nn.sigmoid(projected[:, :, 2 * hidden : 3 * hidden])
        * projected[:, :, 3 * hidden : 4 * hidden]
        * pair_mask
    )
    left_tile = left_tile.astype(jnp.bfloat16).transpose(2, 1, 0)
    right_tile = right_tile.astype(jnp.bfloat16).transpose(2, 1, 0)
    gate_term = jax.nn.sigmoid(projected[:, :, 4 * hidden :])
    right = swap(right_tile)
    left = swap(left_tile)
    right = lax.all_gather(right, "core", axis=0, tiled=False)
    right = right.reshape(2, 4, -1, rows_here)
    left = left.reshape(4, -1, rows_here)
    triangle = jnp.einsum(
        "czkj,bki->bzcji", right, left, preferred_element_type=jnp.float32
    ).astype(jnp.bfloat16)
    triangle = swap(triangle.reshape(hidden, cols_here, rows_here))
    normed_out = layer_norm(
        triangle.astype(jnp.float32), out_gain[:, None, None], out_bias[:, None, None], 0
    ).astype(jnp.bfloat16)
    out_proj = jnp.einsum("hji,hc->ijc", normed_out, out_weight, preferred_element_type=jnp.float32)
    return (gate_term * out_proj).astype(jnp.bfloat16)


def solution(mesh):
    fine = Mesh(mesh.devices.reshape(4, 2, 4, 2, 4), ("zl", "core", "x", "zh", "y"))
    tile = P(("zl", "core"), ("x", "zh", "y"), None)
    placed = (tile, P(), P(), P(), P(), P(), P(), P(), P())
    return jax.shard_map(local, mesh=fine, in_specs=placed, out_specs=tile, check_vma=False)
```

time: 430 us -> 154 us (0.36)
  waiting for transfers between devices: 306 us -> 0.02 us
  blocking collectives: 38.6 us -> 117 us
  starting transfers between devices: 24 us -> 0.04 us
  local copies, waits for them, and re-layouts: 27.8 us -> 6.39 us
    all_to_all x2 -> x0, waiting for transfers between devices: 202 us -> none  [the longest x1 202 us: local(): lax.all_to_all(whole_right, 'col', split_axis=0, concat_axis=2, tiled=True)]
    all_gather x1, waiting for transfers between devices: 104 us -> 0.01 us  [local(): right = lax.all_gather(right, 'core', axis=0, tiled=False)]
    all_to_all x1 -> x3, blocking collectives: 38.6 us -> 117 us  [swap(): lax.all_to_all(chunks, CHIPS, split_axis=0, concat_axis=0, tiled=True)]
    all_to_all x2 -> x0, starting transfers between devices: 24 us -> none  [the longest x1 14.2 us: local(): lax.all_to_all(left_tile, 'col', split_axis=0, concat_axis=2, tiled=True)]
    all_gather x1 -> x0, local copies, waits for them, and re-layouts: 12.4 us -> none  [local(): whole_right = lax.all_gather(right_tile, 'row', axis=1, tiled=True)]
    all_to_all x2 -> x0, local copies, waits for them, and re-layouts: 8.68 us -> none  [the longest x1 8.59 us: local(): lax.all_to_all(whole_right, 'col', split_axis=0, concat_axis=2, tiled=True)]
  transfers between devices with their start and end apart: 3 -> 1, of which waited for: 2 -> 0; matrix products, arithmetic and copies ran while one was open for 3% -> 1% of each run, Pallas kernels for 0% -> 0%
where the time goes in v1:
time: 154 us; the launch traced here: 153 us
  blocking collectives  117 us (76%)
  between operations  13.6 us (9%)
  other arithmetic  9.62 us (6%)
  matrix products  6.99 us (5%)
  local copies, waits for them, and re-layouts  6.39 us (4%)
    all_to_all x3, blocking collectives, swap(): lax.all_to_all(chunks, CHIPS, split_axis=0, concat_axis=0, tiled=True)  117 us
  transfers between devices with their start and end apart: 1, of which 0 were waited for; matrix products, arithmetic and copies ran while one was open for 1% of the time, Pallas kernels for 0%

profile of v1, /device:TPU:8, one launch (start us, length us, event | category | flops | bytes accessed | tf_op | source)
XLA Modules:
  0.0 153.2 jit_solution(1975899295108214350)
XLA Ops:
  6.5 0.0 copy-start
  6.5 0.0 copy-start.2
  6.5 0.0 copy-start.3
  6.5 0.0 copy-start.4
  6.5 0.0 copy-start.5
  6.5 0.0 copy-start.6
  6.6 0.0 all-gather.3.cloned.1.call-start
  6.6 1.9 %convert_reduce_fusion.1 = f32[128,32]{1,0:T(8,128)S(1)} fusion(bf16[128,32,128]{2,1,0:T(8,128)(2,1)} %param.9), kind=kLoop, calls=%fused_computation.3 | loop fusion | flops 1044480 | bytes 1064960 | tf_op jit(solution)/shard_map/reduce_sum | solution.py:11
  8.6 2.3 %fusion.8 = f32[128,32]{1,0:T(8,128)S(1)} fusion(bf16[128,32,128]{2,1,0:T(8,128)(2,1)} %param.9, f32[128,32]{1,0:T(8,128)S(1)} %broadcast_multiply_fusion), kind=kLoop, calls=%fused_computation.12 | loop fusion | flops 2093056 | bytes 1081344 | tf_op jit(solution)/shard_map/reduce_sum | solution.py:13
  10.9 0.0 copy-done.3
  11.0 0.8 dynamic-slice_convert_fusion
  11.8 0.8 dynamic-slice_convert_fusion.1
  12.5 0.0 copy-done.4
  12.5 0.0 copy-done.2
  12.5 0.0 copy-done.5
  12.6 0.0 copy-done.6
  12.6 1.5 fusion.11
  14.1 1.5 fusion.29
  15.6 0.0 copy-start.1
  15.6 0.1 broadcast_multiply_fusion.2
  15.7 1.3 fusion.32
  17.0 2.6 %copy-done.1 = f32[128,32,640]{2,0,1:T(8,128)} copy-done((f32[128,32,640]{2,0,1:T(8,128)}, f32[128,32,640]{2,0,1:T(8,128)S(1)}, u32[]{:S(2)}) %copy-start.1) | copy-done | bytes 10485784
  19.6 1.0 copy.28
  20.6 44.8 %all_to_all.15 = bf16[128,32,128]{2,1,0:T(8,128)(2,1)} all-to-all(bf16[128,32,128]{2,1,0:T(8,128)(2,1)S(1)} %copy.28), channel_id=1, replica_groups=mesh['zl'=4,'core'=2,'x'=4,'zh'=2,'y'=4] {'zl','x','zh','y'}, dimensions={0} | all-to-all | bytes 2097152 | tf_op jit(solution)/shard_map/all_to_all | solution.py:18
  65.4 0.0 all-gather.3.cloned.1.call-update
  65.4 1.0 copy.27
  66.4 36.1 %all_to_all.16 = bf16[128,32,128]{2,1,0:T(8,128)(2,1)S(1)} all-to-all(bf16[128,32,128]{2,1,0:T(8,128)(2,1)S(1)} %copy.27), channel_id=1, replica_groups=mesh['zl'=4,'core'=2,'x'=4,'zh'=2,'y'=4] {'zl','x','zh','y'}, dimensions={0} | all-to-all | bytes 2097152 | tf_op jit(solution)/shard_map/all_to_all | solution.py:18
  102.5 0.0 all-gather.3.cloned.1.call-done
  102.5 2.9 %fusion.27 = bf16[4,4,2,128,128]{4,3,1,2,0:T(8,128)(2,1)S(1)} fusion(bf16[4,1024,128,1,1]{2,1,4,3,0:T(8,128)(2,1)S(1)} %bitcast.36, bf16[2,4,1024,128,1]{3,2,1,0,4:T(8,128)(2,1)} %bitcast.37), kind=kOutput, calls=%fused_computation.37 | convolution fusion | flops 1074266112 | bytes 4194304 | tf_op jit(solution)/shard_map/czkj,bki->bzcji/dot_general | solution.py:64
  105.4 0.1 copy.30
  105.5 0.0 copy-start.7
  105.5 0.0 copy-start.8
  105.5 35.6 %all_to_all.17 = bf16[128,32,128]{2,1,0:T(8,128)(2,1)S(1)} all-to-all(bf16[128,32,128]{2,1,0:T(8,128)(2,1)S(1)} %bitcast.35), channel_id=1, replica_groups=mesh['zl'=4,'core'=2,'x'=4,'zh'=2,'y'=4] {'zl','x','zh','y'}, dimensions={0} | all-to-all | bytes 2097152 | tf_op jit(solution)/shard_map/all_to_all | solution.py:18
  141.1 0.2 convert_reduce_fusion
  141.3 0.3 fusion.4
  141.6 0.0 copy-done.7
  141.7 0.0 copy-done.8
  141.7 0.4 fusion.7
  142.1 0.0 copy-done
  142.1 2.6 %fusion.26 = bf16[128,32,128]{2,0,1:T(8,128)(2,1)S(1)} fusion(f32[128,32,640]{2,0,1:T(8,128)} %copy-done.1, bf16[128,32,128]{2,1,0:T(8,128)(2,1)S(1)} %fusion.7, bf16[128,128]{1,0:T(8,128)(2,1)S(1)} %copy-done), kind=kOutput, calls=%fused_computation.35 | convolution fusion | flops 136839168 | bytes 4227072 | tf_op jit(solution)/shard_map/hji,hc->ijc/dot_general | solution.py:71
  144.7 1.6 %copy.32 = bf16[128,32,128]{2,1,0:T(8,128)(2,1)} copy(bf16[128,32,128]{2,0,1:T(8,128)(2,1)S(1)} %fusion.26) | data formatting | bytes 2097152 | tf_op jit(solution)/shard_map/convert_element_type | solution.py:72
  (9 shorter events, 0.1 us)
Async XLA Ops:
  6.5 135.6 %copy-start = (bf16[128,128]{1,0:T(8,128)(2,1)S(1)}, bf16[128,128]{1,0:T(8,128)(2,1)}, u32[]{:S(2)}) copy-start(bf16[128,128]{1,0:T(8,128)(2,1)} %param.17) | copy-start | bytes 98308
  6.5 6.0 %copy-start.2 = (bf16[128,32,128]{2,1,0:T(8,128)(2,1)S(1)}, bf16[128,32,128]{2,1,0:T(8,128)(2,1)}, u32[]{:S(2)}) copy-start(bf16[128,32,128]{2,1,0:T(8,128)(2,1)} %param.9) | copy-start | bytes 3145732
  6.5 4.4 %copy-start.3 = (bf16[4,128,128]{2,1,0:T(8,128)(2,1)S(1)}, bf16[4,128,128]{2,1,0:T(8,128)(2,1)}, u32[]{:S(2)}) copy-start(bf16[4,128,128]{2,1,0:T(8,128)(2,1)} %param.13) | copy-start | bytes 393220
  6.5 6.0 %copy-start.4 = (bf16[128,128]{1,0:T(8,128)(2,1)S(1)}, bf16[128,128]{1,0:T(8,128)(2,1)}, u32[]{:S(2)}) copy-start(bf16[128,128]{1,0:T(8,128)(2,1)} %param.14) | copy-start | bytes 98308
  6.5 6.0 %copy-start.5 = (f32[128]{0:T(128)S(1)}, f32[128]{0:T(128)}, u32[]{:S(2)}) copy-start(f32[128]{0:T(128)} %param.12) | copy-start | bytes 1540
  6.5 6.0 %copy-start.6 = (f32[128]{0:T(128)S(1)}, f32[128]{0:T(128)}, u32[]{:S(2)}) copy-start(f32[128]{0:T(128)} %param.11) | copy-start | bytes 1540
  6.6 96.0 %all-gather.3.cloned.1.call-start = ((), (), s32[]{:S(2)}) async-start(), calls=%async_computation.3 | async-start | bytes 3145728 | tf_op jit(solution)/shard_map/all_gather | solution.py:61
  15.6 4.0 %copy-start.1 = (f32[128,32,640]{2,0,1:T(8,128)}, f32[128,32,640]{2,0,1:T(8,128)S(1)}, u32[]{:S(2)}) copy-start(f32[128,32,640]{2,0,1:T(8,128)S(1)} %fusion.29) | copy-start | bytes 31457284
  105.5 36.1 %copy-start.7 = (f32[128]{0:T(128)S(1)}, f32[128]{0:T(128)}, u32[]{:S(2)}) copy-start(f32[128]{0:T(128)} %param.16) | copy-start | bytes 1540
  105.5 36.1 %copy-start.8 = (f32[128]{0:T(128)S(1)}, f32[128]{0:T(128)}, u32[]{:S(2)}) copy-start(f32[128]{0:T(128)} %param.15) | copy-start | bytes 1540
Sparse Core Ops, SparseCore 0:
  65.5 11.3 all-gather.2

commit v2 on v1

v2 whole, which is shorter than its diff:
```python
import functools

import jax
import jax.numpy as jnp
from jax import lax
from jax.experimental import pallas as pl
from jax.experimental.pallas import tpu as pltpu
from jax.sharding import Mesh
from jax.sharding import PartitionSpec as P

CHIPS = ("x", "zl", "y", "zh")
VMEM_LIMIT = 40 * 1024 * 1024


def normalise(values, gain_row, bias_row):
    average = jnp.mean(values, axis=-1, keepdims=True)
    centred = values - average
    spread = jnp.mean(centred * centred, axis=-1, keepdims=True)
    return centred * lax.rsqrt(spread + 1e-05) * gain_row + bias_row


def contract(lhs, rhs, lhs_dim, rhs_dim):
    return lax.dot_general(
        lhs, rhs, (((lhs_dim,), (rhs_dim,)), ((), ())), preferred_element_type=jnp.float32
    )


def factors_kernel(
    row_index, col_index, mask_ref, mask_row_ref, x_ref, gain_ref, bias_ref, w_ref, out_ref, xn_ref, xs, ls, rs
):
    rows, part, channels = x_ref.shape
    hidden = w_ref.shape[2]
    step = pl.program_id(0)
    for first in range(0, rows, 16):
        piece = x_ref[first : first + 16].astype(jnp.float32).reshape(16 * part, channels)
        normed = normalise(piece, gain_ref[...], bias_ref[...])
        rounded = normed.astype(jnp.bfloat16)
        xn_ref[first : first + 16] = rounded.reshape(16, part, channels)
        xs[first * part : (first + 16) * part, :] = rounded.astype(jnp.float32)
    weights = jnp.concatenate([w_ref[n].T for n in range(4)], axis=0)
    row_mask = mask_row_ref[pl.ds(row_index(), 1), :].astype(jnp.float32)
    first_col = col_index() * (part * pl.num_programs(0)) + step * part
    for k in range(part):
        of_k = xs[pl.ds(k, rows, stride=part), :].astype(jnp.bfloat16)
        projected = contract(weights, of_k, 1, 1)
        mask = row_mask * mask_ref[first_col + k].astype(jnp.float32)
        left = jax.nn.sigmoid(projected[:hidden]) * projected[hidden : 2 * hidden] * mask
        right = (
            jax.nn.sigmoid(projected[2 * hidden : 3 * hidden]) * projected[3 * hidden :] * mask
        )
        ls[pl.ds(k, hidden, stride=part), :] = left
        rs[pl.ds(k, hidden, stride=part), :] = right
    out_ref[:, 0] = ls[...].reshape(hidden, part, rows).astype(jnp.bfloat16)
    out_ref[:, 1] = rs[...].reshape(hidden, part, rows).astype(jnp.bfloat16)


def row_of():
    return lax.axis_index("zl") * 2 + lax.axis_index("core")


def col_of():
    return (lax.axis_index("x") * 2 + lax.axis_index("zh")) * 4 + lax.axis_index("y")


def factors(pair_rep, residue_mask, in_gain, in_bias, in_weights, row=row_of, col=col_of):
    rows, cols, channels = pair_rep.shape
    hidden = in_weights.shape[2]
    part = 16
    whole = pl.BlockSpec(memory_space=pltpu.VMEM)
    return pl.pallas_call(
        functools.partial(factors_kernel, row, col),
        grid=(cols // part,),
        in_specs=[
            pl.BlockSpec(memory_space=pltpu.SMEM),
            whole,
            pl.BlockSpec((rows, part, channels), lambda s: (0, s, 0)),
            whole,
            whole,
            whole,
        ],
        out_specs=[
            pl.BlockSpec((hidden, 2, part, rows), lambda s: (0, 0, s, 0)),
            pl.BlockSpec((rows, part, channels), lambda s: (0, s, 0)),
        ],
        out_shape=[
            jax.ShapeDtypeStruct((hidden, 2, cols, rows), jnp.bfloat16),
            jax.ShapeDtypeStruct((rows, cols, channels), jnp.bfloat16),
        ],
        scratch_shapes=[
            pltpu.VMEM((rows * part, channels), jnp.float32),
            pltpu.VMEM((hidden * part, rows), jnp.float32),
            pltpu.VMEM((hidden * part, rows), jnp.float32),
        ],
        compiler_params=pltpu.CompilerParams(vmem_limit_bytes=VMEM_LIMIT),
        name="factors",
    )(
        residue_mask,
        residue_mask.reshape(-1, rows),
        pair_rep,
        in_gain.reshape(1, channels),
        in_bias.reshape(1, channels),
        in_weights,
    )


def gate_kernel(x_ref, w_ref, out_ref):
    rows, part, channels = x_ref.shape
    out_ref[...] = jax.nn.sigmoid(
        contract(x_ref[...].reshape(rows * part, channels), w_ref[...], 1, 0)
    ).reshape(rows, part, channels)


def gates(normed_in, gate_weight):
    rows, cols, channels = normed_in.shape
    part = 16
    return pl.pallas_call(
        gate_kernel,
        grid=(rows // part,),
        in_specs=[
            pl.BlockSpec((part, cols, channels), lambda s: (s, 0, 0)),
            pl.BlockSpec(memory_space=pltpu.VMEM),
        ],
        out_specs=pl.BlockSpec((part, cols, channels), lambda s: (s, 0, 0)),
        out_shape=jax.ShapeDtypeStruct((rows, cols, channels), jnp.float32),
        compiler_params=pltpu.CompilerParams(vmem_limit_bytes=VMEM_LIMIT),
        cost_estimate=pl.CostEstimate(
            flops=2 * rows * cols * channels * channels,
            bytes_accessed=6 * rows * cols * channels,
            transcendentals=rows * cols * channels,
        ),
        name="gates",
    )(normed_in, gate_weight)


def product_kernel(core_index, own, left_ref, right_ref, *refs):
    out_ref = refs[-1]
    many_x, many_z = left_ref.shape[:2]
    depth = left_ref.shape[2] * left_ref.shape[3] * left_ref.shape[4]
    wide = left_ref.shape[5]
    core = core_index()
    place = core if own else 1 - core
    for zj in range(many_z):
        rights = jnp.concatenate(
            [right_ref[x, zj].reshape(depth, wide) for x in range(many_x)], axis=0
        )
        lefts = jnp.concatenate(
            [
                jnp.concatenate(
                    [left_ref[x, zi].reshape(depth, wide) for x in range(many_x)], axis=0
                )
                for zi in range(many_z)
            ],
            axis=1,
        )
        out = contract(rights, lefts, 0, 0).astype(jnp.bfloat16)
        for zi in range(many_z):
            out_ref[zj, zi, :, place] = out[:, zi * wide : (zi + 1) * wide].reshape(
                4, wide // 4, wide
            )


def core_of():
    return lax.axis_index("core")


def product(left, right, own, before=None, core=core_of):
    many_x, many_z, many_y, many_h, cols, rows = left.shape
    whole = pl.BlockSpec(memory_space=pltpu.VMEM)
    given = [left, right] if before is None else [left, right, before]
    specs = [whole, whole] if before is None else [whole, whole, pl.BlockSpec(memory_space=pl.ANY)]
    return pl.pallas_call(
        functools.partial(product_kernel, core, own),
        in_specs=specs,
        out_specs=whole,
        out_shape=jax.ShapeDtypeStruct(left.shape, jnp.bfloat16),
        compiler_params=pltpu.CompilerParams(vmem_limit_bytes=VMEM_LIMIT),
        name="product",
    )(*given)


def finish_kernel(t_ref, gate_ref, gain_ref, bias_ref, w_ref, out_ref, ts, os):
    hidden, part, rows = t_ref.shape
    channels = w_ref.shape[1]
    values = t_ref[...].astype(jnp.float32)
    ts[...] = values.reshape(hidden * part, rows)
    average = jnp.sum(values, axis=0) * (1.0 / hidden)
    centred = values - average[None]
    spread = jnp.sum(centred * centred, axis=0) * (1.0 / hidden)
    scale = lax.rsqrt(spread + 1e-05)
    gain = jnp.broadcast_to(gain_ref[...], (hidden, rows))
    bias = jnp.broadcast_to(bias_ref[...], (hidden, rows))
    for j in range(part):
        of_j = ts[pl.ds(j, hidden, stride=part), :]
        normed = (of_j - average[j : j + 1]) * scale[j : j + 1] * gain + bias
        os[pl.ds(j, rows, stride=part), :] = contract(
            normed.astype(jnp.bfloat16), w_ref[...], 0, 0
        )
    out_ref[...] = (os[...].reshape(rows, part, channels) * gate_ref[...]).astype(jnp.bfloat16)


def finish(triangle, gate, out_gain, out_bias, out_weight):
    hidden, cols, rows = triangle.shape
    channels = out_weight.shape[1]
    part = 16
    whole = pl.BlockSpec(memory_space=pltpu.VMEM)
    return pl.pallas_call(
        finish_kernel,
        grid=(cols // part,),
        in_specs=[
            pl.BlockSpec((hidden, part, rows), lambda s: (0, s, 0)),
            pl.BlockSpec((rows, part, channels), lambda s: (0, s, 0)),
            whole,
            whole,
            whole,
        ],
        out_specs=pl.BlockSpec((rows, part, channels), lambda s: (0, s, 0)),
        out_shape=jax.ShapeDtypeStruct((rows, cols, channels), jnp.bfloat16),
        scratch_shapes=[
            pltpu.VMEM((hidden * part, rows), jnp.float32),
            pltpu.VMEM((rows * part, channels), jnp.float32),
        ],
        compiler_params=pltpu.CompilerParams(vmem_limit_bytes=VMEM_LIMIT),
        name="finish",
    )(
        triangle,
        gate,
        out_gain.reshape(hidden, 1),
        out_bias.reshape(hidden, 1),
        out_weight,
    )


def swap(chunks):
    return lax.all_to_all(chunks, CHIPS, split_axis=0, concat_axis=0, tiled=True)


def local(
    pair_rep,
    residue_mask,
    in_gain,
    in_bias,
    in_weights,
    gate_weight,
    out_gain,
    out_bias,
    out_weight,
):
    rows, cols, channels = pair_rep.shape
    hidden = in_weights.shape[2]
    both, normed_in = factors(pair_rep, residue_mask, in_gain, in_bias, in_weights)
    both = swap(both.reshape(hidden, 2 * cols, rows))
    gate = gates(normed_in, gate_weight)
    both = both.reshape(4, 4, 4, 2, 2, cols, rows)
    left, right = both[:, :, :, :, 0], both[:, :, :, :, 1]
    other = lax.ppermute(right, "core", [(0, 1), (1, 0)])
    core = lax.axis_index("core")
    rights = jnp.where(core == 0, jnp.stack([right, other]), jnp.stack([other, right]))
    triangle = jnp.einsum(
        "cxzyhkj,xwyhki->zwcji", rights, left, preferred_element_type=jnp.float32
    ).astype(jnp.bfloat16)
    triangle = triangle.reshape(4, 4, 2, 4, cols, rows).transpose(0, 1, 3, 2, 4, 5)
    triangle = swap(triangle.reshape(hidden, cols, rows))
    return finish(triangle, gate, out_gain, out_bias, out_weight)


def solution(mesh):
    fine = Mesh(mesh.devices.reshape(4, 2, 4, 2, 4), ("zl", "core", "x", "zh", "y"))
    tile = P(("zl", "core"), ("x", "zh", "y"), None)
    placed = (tile, P(), P(), P(), P(), P(), P(), P(), P())
    return jax.shard_map(local, mesh=fine, in_specs=placed, out_specs=tile, check_vma=False)
```

time: 154 us -> 127 us (0.82)
  blocking collectives: 117 us -> 66.8 us
  waiting for transfers between devices: 0.02 us -> 29.9 us
  between operations: 13.6 us -> 0.12 us
  Pallas kernels: 0 us -> 10 us
  other arithmetic: 9.62 us -> 0 us
  starting transfers between devices: 0.04 us -> 8.11 us
  matrix products: 6.99 us -> 2.88 us
    all_to_all x3 -> x1, blocking collectives: 117 us -> 66.8 us  [swap(): lax.all_to_all(chunks, CHIPS, split_axis=0, concat_axis=0, tiled=True)]
    all_to_all x0 -> x1, waiting for transfers between devices: none -> 27.2 us  [swap(): lax.all_to_all(chunks, CHIPS, split_axis=0, concat_axis=0, tiled=True)]
    pallas_call x0 -> x3, Pallas kernels: none -> 10 us  [the longest x1 5.11 us: factors(): pl.pallas_call(functools.partial(factors_kernel, row, col), grid=(cols //...]
    all_to_all x0 -> x1, starting transfers between devices: none -> 8.02 us  [swap(): lax.all_to_all(chunks, CHIPS, split_axis=0, concat_axis=0, tiled=True)]
    reduce_sum x4 -> x0, other arithmetic: 4.76 us -> none  [the longest x2 2.65 us: layer_norm(): spread = jnp.mean(centred * centred, axis=axis_dim, keepdims=True)]
    dot_general x3 -> x1, matrix products: 6.99 us -> 2.88 us  [local(): jnp.einsum('cxzyhkj,xwyhki->zwcji', rights, left, preferred_element_type=...]
    convert_element_type x4 -> x0, other arithmetic: 3.49 us -> none  [the longest x1 1.52 us: local(): layer_norm(pair_rep.astype(jnp.float32), in_gain, in_bias, 2)]
    ppermute x0 -> x1, waiting for transfers between devices: none -> 2.77 us  [local(): other = lax.ppermute(right, 'core', [(0, 1), (1, 0)])]
  transfers between devices with their start and end apart: 1 -> 2, of which waited for: 0 -> 2; matrix products, arithmetic and copies ran while one was open for 1% -> 0% of each run, Pallas kernels for 0% -> 1%
where the time goes in v2:
time: 127 us; the launch traced here: 125 us
  blocking collectives  66.8 us (53%)
  waiting for transfers between devices  29.9 us (24%)
  Pallas kernels  10 us (8%)
  starting transfers between devices  8.11 us (6%)
  local copies, waits for them, and re-layouts  7.64 us (6%)
  matrix products  2.88 us (2%)
    all_to_all x1, blocking collectives, swap(): lax.all_to_all(chunks, CHIPS, split_axis=0, concat_axis=0, tiled=True)  66.8 us
    all_to_all x1, waiting for transfers between devices, swap(): lax.all_to_all(chunks, CHIPS, split_axis=0, concat_axis=0, tiled=True)  27.2 us
    all_to_all x1, starting transfers between devices, swap(): lax.all_to_all(chunks, CHIPS, split_axis=0, concat_axis=0, tiled=True)  8.02 us
    unnamed x22, local copies, waits for them, and re-layouts  5.37 us
    pallas_call x1, Pallas kernels, factors(): pl.pallas_call(functools.partial(factors_kernel, row, col), grid=(cols //...  5.11 us
    pallas_call x1, Pallas kernels, finish(): pl.pallas_call(finish_kernel, grid=(cols // part,), in_specs=[pl.BlockSpe...  3.4 us
    dot_general x1, matrix products, local(): jnp.einsum('cxzyhkj,xwyhki->zwcji', rights, left, preferred_element_type=...  2.88 us
    ppermute x1, waiting for transfers between devices, local(): other = lax.ppermute(right, 'core', [(0, 1), (1, 0)])  2.77 us
  transfers between devices with their start and end apart: 2, of which 2 were waited for; matrix products, arithmetic and copies ran while one was open for 0% of the time, Pallas kernels for 1%

profile of v2, /device:TPU:8, one launch (start us, length us, event | category | flops | bytes accessed | tf_op | source)
XLA Modules:
  0.0 125.5 jit_solution(10590650727617972662)
XLA Ops:
  0.0 0.0 copy-start.2
  0.0 1.2 copy-done.2
  1.2 0.0 copy-start.3
  1.2 0.9 copy-done.3
  2.1 0.0 copy-start.6
  2.1 0.7 copy-done.6
  2.8 0.0 copy-start.7
  2.8 0.7 copy-done.7
  3.5 0.0 copy-start.8
  3.5 0.7 copy-done.8
  4.1 5.1 %factors.1 = (bf16[128,2,32,128]{3,2,1,0:T(8,128)(2,1)S(1)}, bf16[128,32,128]{2,1,0:T(8,128)(2,1)S(1)}) custom-call(s32[1024]{0:T(1024)S(1)} %copy-done.6, s32[8,128]{1,0:T(8,128)S(1)} %bitcast.35, bf16[128,32,128]{2,1,0:T(8,128)(2,1)S(1)} %copy-done.2, f32[1,128]{1,0:T(1,128)S(1)} %bitcast.36, f32[1,128]{1,0:T(1,128)S(1)} %bitcast.37, ...), custom_call_target="tpu_custom_call" | custom-call | tf_op jit(solution)/shard_map/factors/pallas_call | solution.py:70
  9.2 0.0 copy-start
  9.3 66.8 %all_to_all.10 = bf16[128,64,128]{2,1,0:T(8,128)(2,1)S(1)} all-to-all(bf16[128,64,128]{2,1,0:T(8,128)(2,1)S(1)} %bitcast.34), channel_id=1, replica_groups=mesh['zl'=4,'core'=2,'x'=4,'zh'=2,'y'=4] {'x','zl','y','zh'}, dimensions={0} | all-to-all | bytes 4194304 | tf_op jit(solution)/shard_map/all_to_all | solution.py:234
  76.1 0.0 copy-done
  76.1 0.9 fusion.5
  77.0 0.1 collective-permute-start
  77.1 2.8 %collective-permute-done = bf16[4,4,4,2,32,128]{5,4,3,2,1,0:T(8,128)(2,1)} collective-permute-done((bf16[4,4,4,2,32,128]{5,4,3,2,1,0:T(8,128)(2,1)S(1)}, bf16[4,4,4,2,32,128]{5,4,3,2,1,0:T(8,128)(2,1)}, u32[]{:S(2)}, u32[]{:S(2)}) %collective-permute-start) | collective-permute-done | bytes 1048608 | tf_op jit(solution)/shard_map/ppermute | solution.py:255
  79.9 2.9 %bitcast_convert_fusion = bf16[4,128,2,4,128]{1,4,3,2,0:T(8,128)(2,1)S(1)} fusion(bf16[4,4,4,2,1,32,128]{6,5,4,3,2,1,0:T(8,128)(2,1)S(1)} %get-tuple-element.9, bf16[1,4,4,4,2,32,128]{6,5,4,3,2,1,0:T(8,128)(2,1)} %bitcast.10, bf16[1,4,4,4,2,32,128]{6,5,4,3,2,1,0:T(8,128)(2,1)S(1)} %get-tuple-element.11, pred[]{:T(512)S(6)} %eq.3), kind=kOutput, calls=%fused_computation.1 | convolution fusion | flops 1077411840 | bytes 4194305 | tf_op jit(solution)/shard_map/cxzyhkj,xwyhki->zwcji/dot_general | solution.py:258
  82.8 0.0 copy-start.9
  82.8 0.0 copy-start.10
  82.8 0.0 copy-start.4
  82.8 1.1 copy.15
  83.9 8.0 %all-to-all-start.1 = ((bf16[128,32,128]{2,1,0:T(8,128)(2,1)}), bf16[128,32,128]{2,1,0:T(8,128)(2,1)S(1)}, u32[]{:S(2)}, u32[]{:S(2)}) async-start(bf16[128,32,128]{2,1,0:T(8,128)(2,1)} %bitcast.17), calls=%async_computation.1 | async-start | bytes 2097152 | tf_op jit(solution)/shard_map/all_to_all | solution.py:234
  91.9 0.0 copy-start.5
  92.0 0.0 copy-done.9
  92.0 0.1 copy.16.gain_ref
  92.1 0.0 copy-done.10
  92.1 0.1 copy.17.bias_ref
  92.2 0.0 copy-done.4
  92.2 0.0 copy-start.1
  92.2 1.2 copy-done.1
  93.4 1.5 %gates.1.gate_ref = f32[128,32,128]{2,1,0:T(8,128)S(1)} custom-call(bf16[128,32,128]{2,1,0:T(8,128)(2,1)S(1)} %copy-done.1, bf16[128,128]{1,0:T(8,128)(2,1)S(1)} %copy-done.4), custom_call_target="tpu_custom_call" | custom-call | flops 134217728 | bytes 3145728 | tf_op jit(solution)/shard_map/gates/pallas_call | solution.py:116
  94.9 27.2 %all-to-all-done.1.t_ref = bf16[128,32,128]{2,1,0:T(8,128)(2,1)S(1)} async-done(((bf16[128,32,128]{2,1,0:T(8,128)(2,1)}), bf16[128,32,128]{2,1,0:T(8,128)(2,1)S(1)}, u32[]{:S(2)}, u32[]{:S(2)}) %all-to-all-start.1) | async-done | bytes 1048608 | tf_op jit(solution)/shard_map/all_to_all | solution.py:234
  122.1 0.0 copy-done.5
  122.1 3.4 %finish.1 = bf16[128,32,128]{2,1,0:T(8,128)(2,1)} custom-call(bf16[128,32,128]{2,1,0:T(8,128)(2,1)S(1)} %all-to-all-done.1.t_ref, f32[128,32,128]{2,1,0:T(8,128)S(1)} %gates.1.gate_ref, f32[128,1]{1,0:T(8,128)S(1)} %copy.16.gain_ref, f32[128,1]{1,0:T(8,128)S(1)} %copy.17.bias_ref, bf16[128,128]{1,0:T(8,128)(2,1)S(1)} %copy-done.5), custom_call_target="tpu_custom_call" | custom-call | tf_op jit(solution)/shard_map/finish/pallas_call | solution.py:206
Async XLA Ops:
  0.0 1.2 copy-start.2
  1.2 0.9 copy-start.3
  2.1 0.7 copy-start.6
  2.8 0.7 copy-start.7
  3.5 0.7 copy-start.8
  9.2 66.8 %copy-start = (bf16[128,32,128]{2,1,0:T(8,128)(2,1)}, bf16[128,32,128]{2,1,0:T(8,128)(2,1)S(1)}, u32[]{:S(2)}) copy-start(bf16[128,32,128]{2,1,0:T(8,128)(2,1)S(1)} %get-tuple-element.8.x_ref) | copy-start | bytes 3145732
  77.0 2.9 %collective-permute-start = (bf16[4,4,4,2,32,128]{5,4,3,2,1,0:T(8,128)(2,1)S(1)}, bf16[4,4,4,2,32,128]{5,4,3,2,1,0:T(8,128)(2,1)}, u32[]{:S(2)}, u32[]{:S(2)}) collective-permute-start(bf16[4,4,4,2,32,128]{5,4,3,2,1,0:T(8,128)(2,1)S(1)} %get-tuple-element.10), channel_id=1, source_target_pairs={{0,32},{32,0},{1,33},{33,1},{2,34},{34,2},{3,35},{35,3},{4,36},{36... | collective-permute-start | bytes 3145736 | tf_op jit(solution)/shard_map/ppermute | solution.py:255
  82.8 9.2 %copy-start.9 = (f32[128]{0:T(128)S(1)}, f32[128]{0:T(128)}, u32[]{:S(2)}) copy-start(f32[128]{0:T(128)} %param.15) | copy-start | bytes 1540
  82.8 9.3 %copy-start.10 = (f32[128]{0:T(128)S(1)}, f32[128]{0:T(128)}, u32[]{:S(2)}) copy-start(f32[128]{0:T(128)} %param.16) | copy-start | bytes 1540
  82.8 9.4 %copy-start.4 = (bf16[128,128]{1,0:T(8,128)(2,1)S(1)}, bf16[128,128]{1,0:T(8,128)(2,1)}, u32[]{:S(2)}) copy-start(bf16[128,128]{1,0:T(8,128)(2,1)} %w_ref.4) | copy-start | bytes 98308
  83.9 38.2 %all-to-all-start.1 = ((bf16[128,32,128]{2,1,0:T(8,128)(2,1)}), bf16[128,32,128]{2,1,0:T(8,128)(2,1)S(1)}, u32[]{:S(2)}, u32[]{:S(2)}) async-start(bf16[128,32,128]{2,1,0:T(8,128)(2,1)} %bitcast.17), calls=%async_computation.1 | async-start | bytes 2097152 | tf_op jit(solution)/shard_map/all_to_all | solution.py:234
  91.9 30.1 %copy-start.5 = (bf16[128,128]{1,0:T(8,128)(2,1)S(1)}, bf16[128,128]{1,0:T(8,128)(2,1)}, u32[]{:S(2)}) copy-start(bf16[128,128]{1,0:T(8,128)(2,1)} %w_ref.5) | copy-start | bytes 98308
  92.2 1.2 copy-start.1

commit v3 on v2

v3 whole, which is shorter than its diff:
```python
import functools

import jax
import jax.numpy as jnp
from jax import lax
from jax.experimental import pallas as pl
from jax.experimental.pallas import tpu as pltpu
from jax.sharding import Mesh
from jax.sharding import PartitionSpec as P

AXES = ("zl", "core", "x", "zh", "y")
ORDER = ("y0", "z0", "x0", "z2", "y1", "x1", "z1")
VMEM_LIMIT = 60 * 1024 * 1024


def chips():
    places = []
    for place in range(1 << len(ORDER)):
        at = {"z": 0, "x": 0, "y": 0}
        for n, (axis, bit) in enumerate(ORDER):
            at[axis] |= ((place >> (len(ORDER) - 1 - n)) & 1) << int(bit)
        places.append((at["z"], at["x"], at["y"]))
    return places


CHIPS = chips()
PLACE = {chip: place for place, chip in enumerate(CHIPS)}
GROUPS = [
    [(((z % 4 * 2 + core) * 4 + x) * 2 + z // 4) * 4 + y for z, x, y in CHIPS] for core in range(2)
]


def contract(lhs, rhs, lhs_dim, rhs_dim):
    return lax.dot_general(
        lhs, rhs, (((lhs_dim,), (rhs_dim,)), ((), ())), preferred_element_type=jnp.float32
    )


def gated(gate, value):
    return value * pltpu.reciprocal(1.0 + jnp.exp(-gate), approx=True)


def normalise(values, gain_row, bias_row):
    average = jnp.mean(values, axis=-1, keepdims=True)
    centred = values - average
    spread = jnp.mean(centred * centred, axis=-1, keepdims=True)
    return centred * lax.rsqrt(spread + 1e-05) * gain_row + bias_row


def factors_kernel(
    row_index, col_index, mask_ref, mask_row_ref, x_ref, gain_ref, bias_ref, w_ref, out_ref, xn_ref, xs, ls, rs
):
    rows, part, channels = x_ref.shape
    hidden = w_ref.shape[2]
    step = pl.program_id(0)
    for first in range(0, rows, 16):
        piece = x_ref[first : first + 16].astype(jnp.float32).reshape(16 * part, channels)
        normed = normalise(piece, gain_ref[...], bias_ref[...])
        xn_ref[first : first + 16] = normed.astype(jnp.bfloat16).reshape(16, part, channels)
        xs[first * part : (first + 16) * part, :] = normed
    weights = jnp.concatenate([w_ref[n].T for n in range(4)], axis=0)
    row_mask = mask_row_ref[pl.ds(row_index(), 1), :].astype(jnp.float32)
    first_col = col_index() * (part * pl.num_programs(0)) + step * part
    for k in range(part):
        of_k = xs[pl.ds(k, rows, stride=part), :].astype(jnp.bfloat16)
        projected = contract(weights, of_k, 1, 1)
        mask = row_mask * mask_ref[first_col + k].astype(jnp.float32)
        ls[pl.ds(k, hidden, stride=part), :] = (
            gated(projected[:hidden], projected[hidden : 2 * hidden]) * mask
        )
        rs[pl.ds(k, hidden, stride=part), :] = (
            gated(projected[2 * hidden : 3 * hidden], projected[3 * hidden :]) * mask
        )
    out_ref[:, 0] = ls[...].reshape(hidden, part, rows).astype(jnp.bfloat16)
    out_ref[:, 1] = rs[...].reshape(hidden, part, rows).astype(jnp.bfloat16)


def row_of():
    return lax.axis_index("zl") * 2 + lax.axis_index("core")


def col_of():
    return (lax.axis_index("x") * 2 + lax.axis_index("zh")) * 4 + lax.axis_index("y")


def core_of():
    return lax.axis_index("core")


def fixed(shape):
    return pl.BlockSpec(shape, lambda s: (0,) * len(shape))


def factors(pair_rep, residue_mask, in_gain, in_bias, in_weights, row=row_of, col=col_of):
    rows, cols, channels = pair_rep.shape
    hidden = in_weights.shape[2]
    part = 16
    return pl.pallas_call(
        functools.partial(factors_kernel, row, col),
        grid=(cols // part,),
        in_specs=[
            pl.BlockSpec(memory_space=pltpu.SMEM),
            fixed((residue_mask.shape[0] // rows, rows)),
            pl.BlockSpec((rows, part, channels), lambda s: (0, s, 0)),
            fixed((1, channels)),
            fixed((1, channels)),
            fixed(in_weights.shape),
        ],
        out_specs=[
            pl.BlockSpec((hidden, 2, part, rows), lambda s: (0, 0, s, 0)),
            pl.BlockSpec((rows, part, channels), lambda s: (0, s, 0)),
        ],
        out_shape=[
            jax.ShapeDtypeStruct((hidden, 2, cols, rows), jnp.bfloat16),
            jax.ShapeDtypeStruct((rows, cols, channels), jnp.bfloat16),
        ],
        scratch_shapes=[
            pltpu.VMEM((rows * part, channels), jnp.float32),
            pltpu.VMEM((hidden * part, rows), jnp.float32),
            pltpu.VMEM((hidden * part, rows), jnp.float32),
        ],
        compiler_params=pltpu.CompilerParams(vmem_limit_bytes=VMEM_LIMIT),
        name="factors",
    )(
        residue_mask,
        residue_mask.reshape(-1, rows),
        pair_rep,
        in_gain.reshape(1, channels),
        in_bias.reshape(1, channels),
        in_weights,
    )


def gate_kernel(x_ref, w_ref, out_ref):
    rows, part, channels = x_ref.shape
    out_ref[...] = gated(
        contract(x_ref[...].reshape(rows * part, channels), w_ref[...], 1, 0), 1.0
    ).reshape(rows, part, channels)


def gates(normed_in, gate_weight):
    rows, cols, channels = normed_in.shape
    part = 32
    return pl.pallas_call(
        gate_kernel,
        grid=(rows // part,),
        in_specs=[
            pl.BlockSpec((part, cols, channels), lambda s: (s, 0, 0)),
            fixed(gate_weight.shape),
        ],
        out_specs=pl.BlockSpec((part, cols, channels), lambda s: (s, 0, 0)),
        out_shape=jax.ShapeDtypeStruct((rows, cols, channels), jnp.float32),
        compiler_params=pltpu.CompilerParams(vmem_limit_bytes=16 * 1024 * 1024),
        cost_estimate=pl.CostEstimate(
            flops=2 * rows * cols * channels * channels,
            bytes_accessed=6 * rows * cols * channels,
            transcendentals=rows * cols * channels,
        ),
        name="gates",
    )(normed_in, gate_weight)


def blocks(ref, which, zl):
    return jnp.concatenate(
        [
            ref[PLACE[zl + 4 * zh, x, y], which] if which is not None else ref[PLACE[zl + 4 * zh, x, y]]
            for x in range(4)
            for zh in range(2)
            for y in range(4)
        ],
        axis=0,
    )


def half_kernel(both_ref, out_ref):
    lefts = jnp.concatenate([blocks(both_ref, 0, zl) for zl in range(4)], axis=1)
    rights = jnp.concatenate([blocks(both_ref, 1, zl) for zl in range(4)], axis=1)
    out_ref[...] = contract(rights, lefts, 0, 0).astype(jnp.bfloat16)


def product_kernel(core_index, both_ref, right_ref, half_ref, out_ref):
    cols, wide = right_ref.shape[1:]
    core = core_index()
    lefts = jnp.concatenate([blocks(both_ref, 0, zl) for zl in range(4)], axis=1)
    rights = jnp.concatenate([blocks(right_ref, None, zl) for zl in range(4)], axis=1)
    out = contract(rights, lefts, 0, 0).astype(jnp.bfloat16)
    for zl in range(4):
        for x in range(4):
            for y in range(4):
                low, high = PLACE[zl, x, y], PLACE[zl + 4, x, y]
                place = (pl.ds(x * wide + y * cols, cols), pl.ds(zl * wide, wide))
                out_ref[low + core * (high - low)] = half_ref[place]
                out_ref[high + core * (low - high)] = out[
                    x * wide + y * cols : x * wide + (y + 1) * cols, zl * wide : (zl + 1) * wide
                ]


def half(both):
    rows = both.shape[3]
    whole = pl.BlockSpec(memory_space=pltpu.VMEM)
    return pl.pallas_call(
        half_kernel,
        in_specs=[whole],
        out_specs=whole,
        out_shape=jax.ShapeDtypeStruct((4 * rows, 4 * rows), jnp.bfloat16),
        compiler_params=pltpu.CompilerParams(vmem_limit_bytes=24 * 1024 * 1024),
        cost_estimate=pl.CostEstimate(
            flops=2 * 512 * 512 * 1024, bytes_accessed=5 << 19, transcendentals=0
        ),
        name="half",
    )(both)


def product(both, right, own, core=core_of):
    whole = pl.BlockSpec(memory_space=pltpu.VMEM)
    return pl.pallas_call(
        functools.partial(product_kernel, core),
        in_specs=[whole, whole, whole],
        out_specs=whole,
        out_shape=jax.ShapeDtypeStruct(right.shape, jnp.bfloat16),
        compiler_params=pltpu.CompilerParams(vmem_limit_bytes=24 * 1024 * 1024),
        name="product",
    )(both, right, own)


def finish_kernel(t_ref, gate_ref, gain_ref, bias_ref, w_ref, out_ref, ts, os):
    hidden, part, rows = t_ref.shape
    channels = w_ref.shape[1]
    values = t_ref[...].astype(jnp.float32)
    ts[...] = values.reshape(hidden * part, rows)
    average = jnp.sum(values, axis=0) * (1.0 / hidden)
    centred = values - average[None]
    spread = jnp.sum(centred * centred, axis=0) * (1.0 / hidden)
    scale = lax.rsqrt(spread + 1e-05)
    gain = jnp.broadcast_to(gain_ref[...], (hidden, rows))
    bias = jnp.broadcast_to(bias_ref[...], (hidden, rows))
    for j in range(part):
        of_j = ts[pl.ds(j, hidden, stride=part), :]
        normed = (of_j - average[j : j + 1]) * scale[j : j + 1] * gain + bias
        os[pl.ds(j, rows, stride=part), :] = contract(
            normed.astype(jnp.bfloat16), w_ref[...], 0, 0
        )
    out_ref[...] = (os[...].reshape(rows, part, channels) * gate_ref[...]).astype(jnp.bfloat16)


def finish(triangle, gate, out_gain, out_bias, out_weight):
    hidden, cols, rows = triangle.shape
    channels = out_weight.shape[1]
    part = 16
    whole = pl.BlockSpec(memory_space=pltpu.VMEM)
    return pl.pallas_call(
        finish_kernel,
        grid=(cols // part,),
        in_specs=[
            pl.BlockSpec((hidden, part, rows), lambda s: (0, s, 0)),
            pl.BlockSpec((rows, part, channels), lambda s: (0, s, 0)),
            whole,
            whole,
            whole,
        ],
        out_specs=pl.BlockSpec((rows, part, channels), lambda s: (0, s, 0)),
        out_shape=jax.ShapeDtypeStruct((rows, cols, channels), jnp.bfloat16),
        scratch_shapes=[
            pltpu.VMEM((hidden * part, rows), jnp.float32),
            pltpu.VMEM((rows * part, channels), jnp.float32),
        ],
        compiler_params=pltpu.CompilerParams(vmem_limit_bytes=32 * 1024 * 1024),
        name="finish",
    )(
        triangle,
        gate,
        out_gain.reshape(hidden, 1),
        out_bias.reshape(hidden, 1),
        out_weight,
    )


def swap(chunks):
    return lax.all_to_all(
        chunks, AXES, split_axis=0, concat_axis=0, tiled=True, axis_index_groups=GROUPS
    )


def local(
    pair_rep,
    residue_mask,
    in_gain,
    in_bias,
    in_weights,
    gate_weight,
    out_gain,
    out_bias,
    out_weight,
):
    rows, cols, channels = pair_rep.shape
    hidden = in_weights.shape[2]
    both, normed_in = factors(pair_rep, residue_mask, in_gain, in_bias, in_weights)
    both = swap(both.reshape(hidden, 2 * cols, rows)).reshape(hidden, 2, cols, rows)
    right, normed_in = lax.optimization_barrier((both[:, 1], normed_in))
    other = lax.ppermute(right, "core", [(0, 1), (1, 0)])
    own = half(both)
    gate = gates(normed_in, gate_weight)
    other, own, gate = lax.optimization_barrier((other, own, gate))
    triangle = swap(product(both, other, own))
    return finish(triangle, gate, out_gain, out_bias, out_weight)


def solution(mesh):
    fine = Mesh(mesh.devices.reshape(4, 2, 4, 2, 4), AXES)
    tile = P(("zl", "core"), ("x", "zh", "y"), None)
    placed = (tile, P(), P(), P(), P(), P(), P(), P(), P())
    return jax.shard_map(local, mesh=fine, in_specs=placed, out_specs=tile, check_vma=False)
```

time: 127 us -> 121 us (0.953)
  local copies, waits for them, and re-layouts: 7.64 us -> 2.32 us
  matrix products: 2.88 us -> 0 us
  Pallas kernels: 10 us -> 12.5 us
    unnamed x22 -> x12, local copies, waits for them, and re-layouts: 5.37 us -> 2 us
    dot_general x1 -> x0, matrix products: 2.88 us -> none  [local(): jnp.einsum('cxzyhkj,xwyhki->zwcji', rights, left, preferred_element_type=...]
    ppermute x1, waiting for transfers between devices: 2.77 us -> 0.01 us  [local(): other = lax.ppermute(right, 'core', [(0, 1), (1, 0)])]
    all_to_all x1, waiting for transfers between devices: 27.2 us -> 28.7 us  [swap(): lax.all_to_all(chunks, AXES, split_axis=0, concat_axis=0, tiled=True, axi...]
    pallas_call x0 -> x2, Pallas kernels: none -> 1.46 us  [the longest x1 0.74 us: product(): pl.pallas_call(functools.partial(product_kernel, core), in_specs=[whole,...]
    pallas_call x1, Pallas kernels: 5.11 us -> 6.43 us  [factors(): pl.pallas_call(functools.partial(factors_kernel, row, col), grid=(cols //...]
  transfers between devices with their start and end apart: 2 -> 2, of which waited for: 2 -> 1; matrix products, arithmetic and copies ran while one was open for 0% -> 0% of each run, Pallas kernels for 1% -> 2%
where the time goes in v3:
time: 121 us; the launch traced here: 120 us
  blocking collectives  67.2 us (56%)
  waiting for transfers between devices  28.7 us (24%)
  Pallas kernels  12.5 us (10%)
  starting transfers between devices  8.9 us (7%)
  local copies, waits for them, and re-layouts  2.32 us (2%)
    all_to_all x1, blocking collectives, swap(): lax.all_to_all(chunks, AXES, split_axis=0, concat_axis=0, tiled=True, axi...  67.2 us
    all_to_all x1, waiting for transfers between devices, swap(): lax.all_to_all(chunks, AXES, split_axis=0, concat_axis=0, tiled=True, axi...  28.7 us
    all_to_all x1, starting transfers between devices, swap(): lax.all_to_all(chunks, AXES, split_axis=0, concat_axis=0, tiled=True, axi...  8.81 us
    pallas_call x1, Pallas kernels, factors(): pl.pallas_call(functools.partial(factors_kernel, row, col), grid=(cols //...  6.43 us
    pallas_call x1, Pallas kernels, finish(): pl.pallas_call(finish_kernel, grid=(cols // part,), in_specs=[pl.BlockSpe...  3.41 us
  transfers between devices with their start and end apart: 2, of which 1 were waited for; matrix products, arithmetic and copies ran while one was open for 0% of the time, Pallas kernels for 2%

profile of v3, /device:TPU:8, one launch (start us, length us, event | category | flops | bytes accessed | tf_op | source)
XLA Modules:
  0.0 119.7 jit_solution(14439941098298479907)
XLA Ops:
  0.0 6.4 %factors.1 = (bf16[128,2,32,128]{3,2,1,0:T(8,128)(2,1)}, bf16[128,32,128]{2,1,0:T(8,128)(2,1)}) custom-call(s32[1024]{0:T(1024)} %mask_ref.1, s32[8,128]{1,0:T(8,128)} %bitcast.15, bf16[128,32,128]{2,1,0:T(8,128)(2,1)} %x_ref.1, f32[1,128]{1,0:T(1,128)} %bitcast.16, f32[1,128]{1,0:T(1,128)} %bitcast.17, bf16[4,128,128]{2,1,0:T(8,128)(2,1)} %w_ref.3), custom_call_target="tpu_custom_call" | custom-call | tf_op jit(solution)/shard_map/factors/pallas_call | solution.py:98
  6.4 67.2 %all_to_all.10 = bf16[128,64,128]{2,1,0:T(8,128)(2,1)S(1)} all-to-all(bf16[128,64,128]{2,1,0:T(8,128)(2,1)} %bitcast.14), channel_id=1, replica_groups={{0,128,16,144,2,130,18,146,4,132,20,148,6,134,22,150,8,136,24,152,10,13..., dimensions={0} | all-to-all | bytes 4194304 | tf_op jit(solution)/shard_map/all_to_all | solution.py:279
  73.6 0.0 copy-start.1
  73.6 0.0 copy-start.2
  73.6 0.1 slice_bitcast_fusion
  73.7 0.1 collective-permute-start
  73.8 1.0 copy-done.1
  74.8 0.0 copy-done.2
  74.8 1.2 gates.1.gate_ref
  76.0 0.7 half.1.half_ref
  76.8 0.0 collective-permute-done.right_ref
  76.8 0.7 product.1
  77.5 0.0 copy-start
  77.5 1.0 copy-done
  78.5 0.0 copy-start.4
  78.5 0.0 copy-start.5
  78.5 0.0 copy-start.3
  78.5 8.8 %all-to-all-start.1 = ((bf16[128,32,128]{2,1,0:T(8,128)(2,1)}), bf16[128,32,128]{2,1,0:T(8,128)(2,1)S(1)}, u32[]{:S(2)}, u32[]{:S(2)}) async-start(bf16[128,32,128]{2,1,0:T(8,128)(2,1)} %copy-done), calls=%async_computation.1 | async-start | bytes 2097152 | tf_op jit(solution)/shard_map/all_to_all | solution.py:279
  87.3 0.0 copy-done.4
  87.3 0.1 copy.15.gain_ref
  87.4 0.0 copy-done.5
  87.4 0.1 copy.16.bias_ref
  87.6 28.7 %all-to-all-done.1.t_ref = bf16[128,32,128]{2,1,0:T(8,128)(2,1)S(1)} async-done(((bf16[128,32,128]{2,1,0:T(8,128)(2,1)}), bf16[128,32,128]{2,1,0:T(8,128)(2,1)S(1)}, u32[]{:S(2)}, u32[]{:S(2)}) %all-to-all-start.1) | async-done | bytes 1048608 | tf_op jit(solution)/shard_map/all_to_all | solution.py:279
  116.3 0.0 copy-done.3
  116.3 3.4 %finish.1 = bf16[128,32,128]{2,1,0:T(8,128)(2,1)} custom-call(bf16[128,32,128]{2,1,0:T(8,128)(2,1)S(1)} %all-to-all-done.1.t_ref, f32[128,32,128]{2,1,0:T(8,128)S(1)} %gates.1.gate_ref, f32[128,1]{1,0:T(8,128)S(1)} %copy.15.gain_ref, f32[128,1]{1,0:T(8,128)S(1)} %copy.16.bias_ref, bf16[128,128]{1,0:T(8,128)(2,1)S(1)} %copy-done.3), custom_call_target="tpu_custom_call" | custom-call | tf_op jit(solution)/shard_map/finish/pallas_call | solution.py:251
Async XLA Ops:
  73.6 1.2 %copy-start.1 = (bf16[128,32,128]{2,1,0:T(8,128)(2,1)S(1)}, bf16[128,32,128]{2,1,0:T(8,128)(2,1)}, u32[]{:S(2)}) copy-start(bf16[128,32,128]{2,1,0:T(8,128)(2,1)} %get-tuple-element.15.x_ref) | copy-start | bytes 3145732
  73.6 1.2 %copy-start.2 = (bf16[128,128]{1,0:T(8,128)(2,1)S(1)}, bf16[128,128]{1,0:T(8,128)(2,1)}, u32[]{:S(2)}) copy-start(bf16[128,128]{1,0:T(8,128)(2,1)} %w_ref.4) | copy-start | bytes 98308
  73.7 3.0 %collective-permute-start = (bf16[128,32,128]{2,1,0:T(8,128)(2,1)S(1)}, bf16[128,32,128]{2,1,0:T(8,128)(2,1)S(1)}, u32[]{:S(2)}, u32[]{:S(2)}) collective-permute-start(bf16[128,32,128]{2,1,0:T(8,128)(2,1)S(1)} %slice_bitcast_fusion), channel_id=1, source_target_pairs={{0,32},{32,0},{1,33},{33,1},{2,34},{34,2},{3,35},{35,3},{4,36},{36... | collective-permute-start | bytes 3145736 | tf_op jit(solution)/shard_map/ppermute | solution.py:300
  77.5 1.0 copy-start
  78.5 8.8 %copy-start.4 = (f32[128]{0:T(128)S(1)}, f32[128]{0:T(128)}, u32[]{:S(2)}) copy-start(f32[128]{0:T(128)} %param.15) | copy-start | bytes 1540
  78.5 8.9 %copy-start.5 = (f32[128]{0:T(128)S(1)}, f32[128]{0:T(128)}, u32[]{:S(2)}) copy-start(f32[128]{0:T(128)} %param.16) | copy-start | bytes 1540
  78.5 37.8 %copy-start.3 = (bf16[128,128]{1,0:T(8,128)(2,1)S(1)}, bf16[128,128]{1,0:T(8,128)(2,1)}, u32[]{:S(2)}) copy-start(bf16[128,128]{1,0:T(8,128)(2,1)} %w_ref.5) | copy-start | bytes 98308
  78.5 37.8 %all-to-all-start.1 = ((bf16[128,32,128]{2,1,0:T(8,128)(2,1)}), bf16[128,32,128]{2,1,0:T(8,128)(2,1)S(1)}, u32[]{:S(2)}, u32[]{:S(2)}) async-start(bf16[128,32,128]{2,1,0:T(8,128)(2,1)} %copy-done), calls=%async_computation.1 | async-start | bytes 2097152 | tf_op jit(solution)/shard_map/all_to_all | solution.py:279

commit v4 on v3

--- a/solution.py
+++ b/solution.py
@@ -11,6 +11,7 @@
 AXES = ("zl", "core", "x", "zh", "y")
 ORDER = ("y0", "z0", "x0", "z2", "y1", "x1", "z1")
 VMEM_LIMIT = 60 * 1024 * 1024
+APART = 17
 
 
 def chips():
@@ -48,31 +49,63 @@
 
 
 def factors_kernel(
-    row_index, col_index, mask_ref, mask_row_ref, x_ref, gain_ref, bias_ref, w_ref, out_ref, xn_ref, xs, ls, rs
+    row_index, col_index, mask_ref, mask_row_ref, x_hbm, gain_ref, bias_ref, w_hbm, out_hbm, x_ref, w_ref, out_ref, xs, ls, rs, sems
 ):
-    rows, part, channels = x_ref.shape
-    hidden = w_ref.shape[2]
-    step = pl.program_id(0)
-    for first in range(0, rows, 16):
-        piece = x_ref[first : first + 16].astype(jnp.float32).reshape(16 * part, channels)
-        normed = normalise(piece, gain_ref[...], bias_ref[...])
-        xn_ref[first : first + 16] = normed.astype(jnp.bfloat16).reshape(16, part, channels)
-        xs[first * part : (first + 16) * part, :] = normed
-    weights = jnp.concatenate([w_ref[n].T for n in range(4)], axis=0)
+    rows, cols, channels = x_hbm.shape
+    hidden = w_hbm.shape[2]
+    part = 16
+    parts = cols // part
+    copies = [
+        pltpu.make_async_copy(
+            x_hbm.at[:, pl.ds(n * part, part)], x_ref.at[n], sems.at[n]
+        )
+        for n in range(parts)
+    ]
+    load_w = pltpu.make_async_copy(w_hbm, w_ref, sems.at[parts])
+    load_w.start()
+    for copy in copies:
+        copy.start()
+    load_w.wait()
+    weights = jnp.concatenate([w_ref[m].T for m in range(4)], axis=0)
+    stores = []
     row_mask = mask_row_ref[pl.ds(row_index(), 1), :].astype(jnp.float32)
-    first_col = col_index() * (part * pl.num_programs(0)) + step * part
-    for k in range(part):
-        of_k = xs[pl.ds(k, rows, stride=part), :].astype(jnp.bfloat16)
-        projected = contract(weights, of_k, 1, 1)
-        mask = row_mask * mask_ref[first_col + k].astype(jnp.float32)
-        ls[pl.ds(k, hidden, stride=part), :] = (
-            gated(projected[:hidden], projected[hidden : 2 * hidden]) * mask
+    first_col = col_index() * cols
+    for n in range(parts):
+        copies[n].wait()
+        for first in range(0, rows, 16):
+            piece = x_ref[n, first : first + 16].astype(jnp.float32).reshape(16 * part, channels)
+            normed = normalise(piece, gain_ref[...], bias_ref[...])
+            for i in range(16):
+                xs[(first + i) * APART : (first + i) * APART + part, :] = normed[i * part : (i + 1) * part]
+        for k in range(0, part, 2):
+            of_k = jnp.concatenate(
+                [xs[pl.ds(k + d, rows, stride=APART), :].astype(jnp.bfloat16) for d in range(2)],
+                axis=0,
+            )
+            projected = contract(weights, of_k, 1, 1)
+            for d in range(2):
+                mine = projected[:, d * rows : (d + 1) * rows]
+                mask = row_mask * mask_ref[first_col + n * part + k + d].astype(jnp.float32)
+                ls[pl.ds(k + d, hidden, stride=APART), :] = (
+                    gated(mine[:hidden], mine[hidden : 2 * hidden]) * mask
+                )
+                rs[pl.ds(k + d, hidden, stride=APART), :] = (
+                    gated(mine[2 * hidden : 3 * hidden], mine[3 * hidden :]) * mask
+                )
+        here = slice(n * part, (n + 1) * part)
+        for h in range(hidden):
+            out_ref[h, 0, here] = ls[h * APART : h * APART + part].astype(jnp.bfloat16)
+            out_ref[h, 1, here] = rs[h * APART : h * APART + part].astype(jnp.bfloat16)
+        stores.append(
+            pltpu.make_async_copy(
+                out_ref.at[:, :, pl.ds(n * part, part)],
+                out_hbm.at[:, :, pl.ds(n * part, part)],
+                sems.at[parts + 1 + n],
+            )
         )
-        rs[pl.ds(k, hidden, stride=part), :] = (
-            gated(projected[2 * hidden : 3 * hidden], projected[3 * hidden :]) * mask
-        )
-    out_ref[:, 0] = ls[...].reshape(hidden, part, rows).astype(jnp.bfloat16)
-    out_ref[:, 1] = rs[...].reshape(hidden, part, rows).astype(jnp.bfloat16)
+        stores[-1].start()
+    for store in stores:
+        store.wait()
 
 
 def row_of():
@@ -95,29 +128,21 @@
     rows, cols, channels = pair_rep.shape
     hidden = in_weights.shape[2]
     part = 16
+    whole = pl.BlockSpec(memory_space=pltpu.VMEM)
+    far = pl.BlockSpec(memory_space=pltpu.HBM)
     return pl.pallas_call(
         functools.partial(factors_kernel, row, col),
-        grid=(cols // part,),
-        in_specs=[
-            pl.BlockSpec(memory_space=pltpu.SMEM),
-            fixed((residue_mask.shape[0] // rows, rows)),
-            pl.BlockSpec((rows, part, channels), lambda s: (0, s, 0)),
-            fixed((1, channels)),
-            fixed((1, channels)),
-            fixed(in_weights.shape),
-        ],
-        out_specs=[
-            pl.BlockSpec((hidden, 2, part, rows), lambda s: (0, 0, s, 0)),
-            pl.BlockSpec((rows, part, channels), lambda s: (0, s, 0)),
-        ],
-        out_shape=[
-            jax.ShapeDtypeStruct((hidden, 2, cols, rows), jnp.bfloat16),
-            jax.ShapeDtypeStruct((rows, cols, channels), jnp.bfloat16),
-        ],
+        in_specs=[pl.BlockSpec(memory_space=pltpu.SMEM), whole, far, whole, whole, far],
+        out_specs=far,
+        out_shape=jax.ShapeDtypeStruct((hidden, 2, cols, rows), jnp.bfloat16),
         scratch_shapes=[
-            pltpu.VMEM((rows * part, channels), jnp.float32),
-            pltpu.VMEM((hidden * part, rows), jnp.float32),
-            pltpu.VMEM((hidden * part, rows), jnp.float32),
+            pltpu.VMEM((cols // part, rows, part, channels), jnp.bfloat16),
+            pltpu.VMEM(in_weights.shape, jnp.bfloat16),
+            pltpu.VMEM((hidden, 2, cols, rows), jnp.bfloat16),
+            pltpu.VMEM((rows * APART, channels), jnp.float32),
+            pltpu.VMEM((hidden * APART, rows), jnp.float32),
+            pltpu.VMEM((hidden * APART, rows), jnp.float32),
+            pltpu.SemaphoreType.DMA((2 * (cols // part) + 1,)),
         ],
         compiler_params=pltpu.CompilerParams(vmem_limit_bytes=VMEM_LIMIT),
         name="factors",
@@ -131,24 +156,22 @@
     )
 
 
-def gate_kernel(x_ref, w_ref, out_ref):
-    rows, part, channels = x_ref.shape
-    out_ref[...] = gated(
-        contract(x_ref[...].reshape(rows * part, channels), w_ref[...], 1, 0), 1.0
-    ).reshape(rows, part, channels)
-
-
-def gates(normed_in, gate_weight):
-    rows, cols, channels = normed_in.shape
-    part = 32
+def gate_kernel(x_ref, gain_ref, bias_ref, w_ref, out_ref):
+    rows, cols, channels = x_ref.shape
+    values = x_ref[...].astype(jnp.float32).reshape(rows * cols, channels)
+    normed = normalise(values, gain_ref[...], bias_ref[...]).astype(jnp.bfloat16)
+    out_ref[...] = gated(contract(normed, w_ref[...], 1, 0), 1.0).reshape(rows, cols, channels)
+
+
+def gates(pair_rep, in_gain, in_bias, gate_weight):
+    rows, cols, channels = pair_rep.shape
+    part = 16
+    block = pl.BlockSpec((part, cols, channels), lambda s: (s, 0, 0))
     return pl.pallas_call(
         gate_kernel,
         grid=(rows // part,),
-        in_specs=[
-            pl.BlockSpec((part, cols, channels), lambda s: (s, 0, 0)),
-            fixed(gate_weight.shape),
-        ],
-        out_specs=pl.BlockSpec((part, cols, channels), lambda s: (s, 0, 0)),
+        in_specs=[block, fixed((1, channels)), fixed((1, channels)), fixed(gate_weight.shape)],
+        out_specs=block,
         out_shape=jax.ShapeDtypeStruct((rows, cols, channels), jnp.float32),
         compiler_params=pltpu.CompilerParams(vmem_limit_bytes=16 * 1024 * 1024),
         cost_estimate=pl.CostEstimate(
@@ -157,7 +180,7 @@
             transcendentals=rows * cols * channels,
         ),
         name="gates",
-    )(normed_in, gate_weight)
+    )(pair_rep, in_gain.reshape(1, channels), in_bias.reshape(1, channels), gate_weight)
 
 
 def blocks(ref, which, zl):
@@ -227,20 +250,22 @@
     hidden, part, rows = t_ref.shape
     channels = w_ref.shape[1]
     values = t_ref[...].astype(jnp.float32)
-    ts[...] = values.reshape(hidden * part, rows)
+    for h in range(hidden):
+        ts[h * APART : h * APART + part, :] = values[h]
     average = jnp.sum(values, axis=0) * (1.0 / hidden)
     centred = values - average[None]
     spread = jnp.sum(centred * centred, axis=0) * (1.0 / hidden)
     scale = lax.rsqrt(spread + 1e-05)
-    gain = jnp.broadcast_to(gain_ref[...], (hidden, rows))
-    bias = jnp.broadcast_to(bias_ref[...], (hidden, rows))
+    gain = jnp.broadcast_to(gain_ref[...], (rows, hidden)).T
+    bias = jnp.broadcast_to(bias_ref[...], (rows, hidden)).T
     for j in range(part):
-        of_j = ts[pl.ds(j, hidden, stride=part), :]
+        of_j = ts[pl.ds(j, hidden, stride=APART), :]
         normed = (of_j - average[j : j + 1]) * scale[j : j + 1] * gain + bias
-        os[pl.ds(j, rows, stride=part), :] = contract(
+        os[pl.ds(j, rows, stride=APART), :] = contract(
             normed.astype(jnp.bfloat16), w_ref[...], 0, 0
         )
-    out_ref[...] = (os[...].reshape(rows, part, channels) * gate_ref[...]).astype(jnp.bfloat16)
+    for i in range(rows):
+        out_ref[i] = (os[i * APART : i * APART + part, :] * gate_ref[i]).astype(jnp.bfloat16)
 
 
 def finish(triangle, gate, out_gain, out_bias, out_weight):
@@ -261,16 +286,16 @@
         out_specs=pl.BlockSpec((rows, part, channels), lambda s: (0, s, 0)),
         out_shape=jax.ShapeDtypeStruct((rows, cols, channels), jnp.bfloat16),
         scratch_shapes=[
-            pltpu.VMEM((hidden * part, rows), jnp.float32),
-            pltpu.VMEM((rows * part, channels), jnp.float32),
+            pltpu.VMEM((hidden * APART, rows), jnp.float32),
+            pltpu.VMEM((rows * APART, channels), jnp.float32),
         ],
         compiler_params=pltpu.CompilerParams(vmem_limit_bytes=32 * 1024 * 1024),
         name="finish",
     )(
         triangle,
         gate,
-        out_gain.reshape(hidden, 1),
-        out_bias.reshape(hidden, 1),
+        out_gain.reshape(1, hidden),
+        out_bias.reshape(1, hidden),
         out_weight,
     )
 
@@ -294,13 +319,13 @@
 ):
     rows, cols, channels = pair_rep.shape
     hidden = in_weights.shape[2]
-    both, normed_in = factors(pair_rep, residue_mask, in_gain, in_bias, in_weights)
+    both = factors(pair_rep, residue_mask, in_gain, in_bias, in_weights)
+    both, late = lax.optimization_barrier((both, pair_rep))
     both = swap(both.reshape(hidden, 2 * cols, rows)).reshape(hidden, 2, cols, rows)
-    right, normed_in = lax.optimization_barrier((both[:, 1], normed_in))
-    other = lax.ppermute(right, "core", [(0, 1), (1, 0)])
+    gate = gates(late, in_gain, in_bias, gate_weight)
+    both, gate = lax.optimization_barrier((both, gate))
+    other = lax.ppermute(both[:, 1], "core", [(0, 1), (1, 0)])
     own = half(both)
-    gate = gates(normed_in, gate_weight)
-    other, own, gate = lax.optimization_barrier((other, own, gate))
     triangle = swap(product(both, other, own))
     return finish(triangle, gate, out_gain, out_bias, out_weight)
 

time: 121 us -> 118 us (0.975)
  blocking collectives: 67.2 us -> 37.9 us
  waiting for transfers between devices: 28.7 us -> 49 us
  starting transfers between devices: 8.9 us -> 15.9 us
    all_to_all x1, blocking collectives: 67.2 us -> 37.9 us  [swap(): lax.all_to_all(chunks, AXES, split_axis=0, concat_axis=0, tiled=True, axi...]
    all_to_all x1, waiting for transfers between devices: 28.7 us -> 47.1 us  [swap(): lax.all_to_all(chunks, AXES, split_axis=0, concat_axis=0, tiled=True, axi...]
    all_to_all x1, starting transfers between devices: 8.81 us -> 15.8 us  [swap(): lax.all_to_all(chunks, AXES, split_axis=0, concat_axis=0, tiled=True, axi...]
    ppermute x1, waiting for transfers between devices: 0.01 us -> 1.91 us  [local(): other = lax.ppermute(both[:, 1], 'core', [(0, 1), (1, 0)])]
    pallas_call x2, Pallas kernels: 7.6 us -> 8.85 us  [the longest x1 5.77 us: factors(): pl.pallas_call(functools.partial(factors_kernel, row, col), in_specs=[pl....]
  transfers between devices with their start and end apart: 2 -> 2, of which waited for: 1 -> 2; matrix products, arithmetic and copies ran while one was open for 0% -> 0% of each run, Pallas kernels for 2% -> 3%
where the time goes in v4:
time: 118 us; the launch traced here: 117 us
  waiting for transfers between devices  49 us (42%)
  blocking collectives  37.9 us (32%)
  starting transfers between devices  15.9 us (13%)
  Pallas kernels  13 us (11%)
  local copies, waits for them, and re-layouts  1.46 us (1%)
    all_to_all x1, waiting for transfers between devices, swap(): lax.all_to_all(chunks, AXES, split_axis=0, concat_axis=0, tiled=True, axi...  47.1 us
    all_to_all x1, blocking collectives, swap(): lax.all_to_all(chunks, AXES, split_axis=0, concat_axis=0, tiled=True, axi...  37.9 us
    all_to_all x1, starting transfers between devices, swap(): lax.all_to_all(chunks, AXES, split_axis=0, concat_axis=0, tiled=True, axi...  15.8 us
    pallas_call x1, Pallas kernels, factors(): pl.pallas_call(functools.partial(factors_kernel, row, col), in_specs=[pl....  5.77 us
    pallas_call x1, Pallas kernels, gates(): pl.pallas_call(gate_kernel, grid=(rows // part,), in_specs=[block, fixed(...  3.07 us
    pallas_call x1, Pallas kernels, finish(): pl.pallas_call(finish_kernel, grid=(cols // part,), in_specs=[pl.BlockSpe...  2.65 us
  transfers between devices with their start and end apart: 2, of which 2 were waited for; matrix products, arithmetic and copies ran while one was open for 0% of the time, Pallas kernels for 3%

profile of v4, /device:TPU:8, one launch (start us, length us, event | category | flops | bytes accessed | tf_op | source)
XLA Modules:
  0.0 117.4 jit_solution(11131360633025866215)
XLA Ops:
  0.0 5.8 %factors.1 = bf16[128,2,32,128]{3,2,1,0:T(8,128)(2,1)} custom-call(s32[1024]{0:T(1024)} %mask_ref.1, s32[8,128]{1,0:T(8,128)} %bitcast.19, bf16[128,32,128]{2,1,0:T(8,128)(2,1)} %x_ref, f32[1,128]{1,0:T(1,128)} %bitcast.12, f32[1,128]{1,0:T(1,128)} %bitcast.14, bf16[4,128,128]{2,1,0:T(8,128)(2,1)} %w_hbm.1), custom_call_target="tpu_custom_call" | custom-call | tf_op jit(solution)/shard_map/factors/pallas_call | solution.py:133
  5.8 0.0 copy-start.2
  5.8 0.0 copy-start.3
  5.8 0.0 copy-start.5
  5.8 0.0 copy-start.6
  5.8 15.8 %all-to-all-start = ((bf16[128,64,128]{2,1,0:T(8,128)(2,1)}), bf16[128,64,128]{2,1,0:T(8,128)(2,1)S(1)}, u32[]{:S(2)}, u32[]{:S(2)}) async-start(bf16[128,64,128]{2,1,0:T(8,128)(2,1)} %bitcast.18), calls=%async_computation | async-start | bytes 4194304 | tf_op jit(solution)/shard_map/all_to_all | solution.py:304
  21.6 0.0 copy-done.2
  21.7 0.0 copy-done.3
  21.7 0.0 copy-done.5
  21.7 0.0 copy-done.6
  21.7 3.1 %gates.1.gate_ref = f32[128,32,128]{2,1,0:T(8,128)S(1)} custom-call(bf16[128,32,128]{2,1,0:T(8,128)(2,1)S(1)} %copy-done.2, f32[1,128]{1,0:T(1,128)S(1)} %bitcast.13, f32[1,128]{1,0:T(1,128)S(1)} %bitcast.15, bf16[128,128]{1,0:T(8,128)(2,1)S(1)} %copy-done.3), custom_call_target="tpu_custom_call" | custom-call | flops 134217728 | bytes 3145728 | tf_op jit(solution)/shard_map/gates/pallas_call | solution.py:170
  24.8 0.0 copy-start
  24.8 1.3 %copy-done = f32[128,32,128]{2,1,0:T(8,128)} copy-done((f32[128,32,128]{2,1,0:T(8,128)}, f32[128,32,128]{2,1,0:T(8,128)S(1)}, u32[]{:S(2)}) %copy-start) | copy-done | bytes 2097176
  26.1 47.1 %all-to-all-done = bf16[128,64,128]{2,1,0:T(8,128)(2,1)S(1)} async-done(((bf16[128,64,128]{2,1,0:T(8,128)(2,1)}), bf16[128,64,128]{2,1,0:T(8,128)(2,1)S(1)}, u32[]{:S(2)}, u32[]{:S(2)}) %all-to-all-start) | async-done | bytes 2097184 | tf_op jit(solution)/shard_map/all_to_all | solution.py:304
  73.2 0.1 slice_bitcast_fusion
  73.3 0.1 collective-permute-start
  73.4 0.7 half.1.half_ref
  74.1 1.9 %collective-permute-done.right_ref = bf16[128,32,128]{2,1,0:T(8,128)(2,1)S(1)} collective-permute-done((bf16[128,32,128]{2,1,0:T(8,128)(2,1)S(1)}, bf16[128,32,128]{2,1,0:T(8,128)(2,1)S(1)}, u32[]{:S(2)}, u32[]{:S(2)}) %collective-permute-start) | collective-permute-done | bytes 1048608 | tf_op jit(solution)/shard_map/ppermute | solution.py:327
  76.0 0.0 copy-start.4
  76.0 0.7 product.1
  76.8 0.0 copy-start.1
  76.8 0.0 copy-start.7
  76.8 0.0 copy-start.8
  76.8 37.9 %all_to_all.10.t_ref = bf16[128,32,128]{2,1,0:T(8,128)(2,1)S(1)} all-to-all(bf16[128,32,128]{2,1,0:T(8,128)(2,1)S(1)} %product.1), channel_id=1, replica_groups={{0,128,16,144,2,130,18,146,4,132,20,148,6,134,22,150,8,136,24,152,10,13..., dimensions={0} | all-to-all | bytes 2097152 | tf_op jit(solution)/shard_map/all_to_all | solution.py:304
  114.7 0.0 copy-done.4
  114.7 0.0 copy-done.1
  114.8 0.0 copy-done.7
  114.8 0.0 copy-done.8
  114.8 2.6 %finish.1 = bf16[128,32,128]{2,1,0:T(8,128)(2,1)} custom-call(bf16[128,32,128]{2,1,0:T(8,128)(2,1)S(1)} %all_to_all.10.t_ref, f32[128,32,128]{2,1,0:T(8,128)S(1)} %copy-done.1, f32[1,128]{1,0:T(1,128)S(1)} %bitcast.16, f32[1,128]{1,0:T(1,128)S(1)} %bitcast.17, bf16[128,128]{1,0:T(8,128)(2,1)S(1)} %copy-done.4), custom_call_target="tpu_custom_call" | custom-call | tf_op jit(solution)/shard_map/finish/pallas_call | solution.py:276
Async XLA Ops:
  5.8 15.9 %copy-start.2 = (bf16[128,32,128]{2,1,0:T(8,128)(2,1)S(1)}, bf16[128,32,128]{2,1,0:T(8,128)(2,1)}, u32[]{:S(2)}) copy-start(bf16[128,32,128]{2,1,0:T(8,128)(2,1)} %x_ref) | copy-start | bytes 3145732
  5.8 15.9 %copy-start.3 = (bf16[128,128]{1,0:T(8,128)(2,1)S(1)}, bf16[128,128]{1,0:T(8,128)(2,1)}, u32[]{:S(2)}) copy-start(bf16[128,128]{1,0:T(8,128)(2,1)} %w_ref.2) | copy-start | bytes 98308
  5.8 15.9 %copy-start.5 = (f32[128]{0:T(128)S(1)}, f32[128]{0:T(128)}, u32[]{:S(2)}) copy-start(f32[128]{0:T(128)} %param.11) | copy-start | bytes 1540
  5.8 15.9 %copy-start.6 = (f32[128]{0:T(128)S(1)}, f32[128]{0:T(128)}, u32[]{:S(2)}) copy-start(f32[128]{0:T(128)} %param.12) | copy-start | bytes 1540
  5.8 67.3 %all-to-all-start = ((bf16[128,64,128]{2,1,0:T(8,128)(2,1)}), bf16[128,64,128]{2,1,0:T(8,128)(2,1)S(1)}, u32[]{:S(2)}, u32[]{:S(2)}) async-start(bf16[128,64,128]{2,1,0:T(8,128)(2,1)} %bitcast.18), calls=%async_computation | async-start | bytes 4194304 | tf_op jit(solution)/shard_map/all_to_all | solution.py:304
  24.8 1.3 %copy-start = (f32[128,32,128]{2,1,0:T(8,128)}, f32[128,32,128]{2,1,0:T(8,128)S(1)}, u32[]{:S(2)}) copy-start(f32[128,32,128]{2,1,0:T(8,128)S(1)} %gates.1.gate_ref) | copy-start | bytes 6291460
  73.3 2.7 %collective-permute-start = (bf16[128,32,128]{2,1,0:T(8,128)(2,1)S(1)}, bf16[128,32,128]{2,1,0:T(8,128)(2,1)S(1)}, u32[]{:S(2)}, u32[]{:S(2)}) collective-permute-start(bf16[128,32,128]{2,1,0:T(8,128)(2,1)S(1)} %slice_bitcast_fusion), channel_id=1, source_target_pairs={{0,32},{32,0},{1,33},{33,1},{2,34},{34,2},{3,35},{35,3},{4,36},{36... | collective-permute-start | bytes 3145736 | tf_op jit(solution)/shard_map/ppermute | solution.py:327
  76.0 38.7 %copy-start.4 = (bf16[128,128]{1,0:T(8,128)(2,1)S(1)}, bf16[128,128]{1,0:T(8,128)(2,1)}, u32[]{:S(2)}) copy-start(bf16[128,128]{1,0:T(8,128)(2,1)} %w_ref.3) | copy-start | bytes 98308
  76.8 38.0 %copy-start.1 = (f32[128,32,128]{2,1,0:T(8,128)S(1)}, f32[128,32,128]{2,1,0:T(8,128)}, u32[]{:S(2)}) copy-start(f32[128,32,128]{2,1,0:T(8,128)} %copy-done) | copy-start | bytes 6291460
  76.8 38.0 %copy-start.7 = (f32[128]{0:T(128)S(1)}, f32[128]{0:T(128)}, u32[]{:S(2)}) copy-start(f32[128]{0:T(128)} %param.15) | copy-start | bytes 1540
  76.8 38.0 %copy-start.8 = (f32[128]{0:T(128)S(1)}, f32[128]{0:T(128)}, u32[]{:S(2)}) copy-start(f32[128]{0:T(128)} %param.16) | copy-start | bytes 1540

commit v5 on v4

--- a/solution.py
+++ b/solution.py
@@ -9,7 +9,7 @@
 from jax.sharding import PartitionSpec as P
 
 AXES = ("zl", "core", "x", "zh", "y")
-ORDER = ("y0", "z0", "x0", "z2", "y1", "x1", "z1")
+ORDER = ("z1", "x1", "y1", "z2", "z0", "x0", "y0")
 VMEM_LIMIT = 60 * 1024 * 1024
 APART = 17
 
@@ -20,7 +20,7 @@
         at = {"z": 0, "x": 0, "y": 0}
         for n, (axis, bit) in enumerate(ORDER):
             at[axis] |= ((place >> (len(ORDER) - 1 - n)) & 1) << int(bit)
-        places.append((at["z"], at["x"], at["y"]))
+        places.append((7 - at["z"], 3 - at["x"], 3 - at["y"]))
     return places
 
 
@@ -246,26 +246,42 @@
     )(both, right, own)
 
 
-def finish_kernel(t_ref, gate_ref, gain_ref, bias_ref, w_ref, out_ref, ts, os):
-    hidden, part, rows = t_ref.shape
+def finish_kernel(t_ref, gate_ref, gain_ref, bias_ref, w_ref, out_hbm, out_ref, ts, os, sems):
+    hidden, cols, rows = t_ref.shape
     channels = w_ref.shape[1]
-    values = t_ref[...].astype(jnp.float32)
-    for h in range(hidden):
-        ts[h * APART : h * APART + part, :] = values[h]
-    average = jnp.sum(values, axis=0) * (1.0 / hidden)
-    centred = values - average[None]
-    spread = jnp.sum(centred * centred, axis=0) * (1.0 / hidden)
-    scale = lax.rsqrt(spread + 1e-05)
+    part = 16
     gain = jnp.broadcast_to(gain_ref[...], (rows, hidden)).T
     bias = jnp.broadcast_to(bias_ref[...], (rows, hidden)).T
-    for j in range(part):
-        of_j = ts[pl.ds(j, hidden, stride=APART), :]
-        normed = (of_j - average[j : j + 1]) * scale[j : j + 1] * gain + bias
-        os[pl.ds(j, rows, stride=APART), :] = contract(
-            normed.astype(jnp.bfloat16), w_ref[...], 0, 0
-        )
-    for i in range(rows):
-        out_ref[i] = (os[i * APART : i * APART + part, :] * gate_ref[i]).astype(jnp.bfloat16)
+    stores = []
+    for n in range(cols // part):
+        here = slice(n * part, (n + 1) * part)
+        values = t_ref[:, here].astype(jnp.float32)
+        for h in range(hidden):
+            ts[h * APART : h * APART + part, :] = values[h]
+        average = jnp.sum(values, axis=0) * (1.0 / hidden)
+        centred = values - average[None]
+        spread = jnp.sum(centred * centred, axis=0) * (1.0 / hidden)
+        scale = lax.rsqrt(spread + 1e-05)
+        for j in range(part):
+            of_j = ts[pl.ds(j, hidden, stride=APART), :]
+            normed = (of_j - average[j : j + 1]) * scale[j : j + 1] * gain + bias
+            os[pl.ds(j, rows, stride=APART), :] = contract(
+                normed.astype(jnp.bfloat16), w_ref[...], 0, 0
+            )
+        for i in range(rows):
+            out_ref[i, here] = (
+                os[i * APART : i * APART + part, :] * gate_ref[i, here]
+            ).astype(jnp.bfloat16)
+            if (i + 1) % 64 == 0:
+                some = (pl.ds(i - 63, 64), pl.ds(n * part, part))
+                stores.append(
+                    pltpu.make_async_copy(
+                        out_ref.at[some], out_hbm.at[some], sems.at[len(stores)]
+                    )
+                )
+                stores[-1].start()
+    for store in stores:
+        store.wait()
 
 
 def finish(triangle, gate, out_gain, out_bias, out_weight):
@@ -275,19 +291,14 @@
     whole = pl.BlockSpec(memory_space=pltpu.VMEM)
     return pl.pallas_call(
         finish_kernel,
-        grid=(cols // part,),
-        in_specs=[
-            pl.BlockSpec((hidden, part, rows), lambda s: (0, s, 0)),
-            pl.BlockSpec((rows, part, channels), lambda s: (0, s, 0)),
-            whole,
-            whole,
-            whole,
-        ],
-        out_specs=pl.BlockSpec((rows, part, channels), lambda s: (0, s, 0)),
+        in_specs=[whole] * 5,
+        out_specs=pl.BlockSpec(memory_space=pltpu.HBM),
         out_shape=jax.ShapeDtypeStruct((rows, cols, channels), jnp.bfloat16),
         scratch_shapes=[
+            pltpu.VMEM((rows, cols, channels), jnp.bfloat16),
             pltpu.VMEM((hidden * APART, rows), jnp.float32),
             pltpu.VMEM((rows * APART, channels), jnp.float32),
+            pltpu.SemaphoreType.DMA((2 * (cols // part),)),
         ],
         compiler_params=pltpu.CompilerParams(vmem_limit_bytes=32 * 1024 * 1024),
         name="finish",

time: 118 us -> 113 us (0.958)
  waiting for transfers between devices: 49 us -> 43.5 us
    all_to_all x1, waiting for transfers between devices: 47.1 us -> 41.6 us  [swap(): lax.all_to_all(chunks, AXES, split_axis=0, concat_axis=0, tiled=True, axi...]
where the time goes in v5:
time: 113 us; the launch traced here: 112 us
  waiting for transfers between devices  43.5 us (38%)
  blocking collectives  37.5 us (33%)
  starting transfers between devices  16.8 us (15%)
  Pallas kernels  12.7 us (11%)
  local copies, waits for them, and re-layouts  1.46 us (1%)
    all_to_all x1, waiting for transfers between devices, swap(): lax.all_to_all(chunks, AXES, split_axis=0, concat_axis=0, tiled=True, axi...  41.6 us
    all_to_all x1, blocking collectives, swap(): lax.all_to_all(chunks, AXES, split_axis=0, concat_axis=0, tiled=True, axi...  37.5 us
    all_to_all x1, starting transfers between devices, swap(): lax.all_to_all(chunks, AXES, split_axis=0, concat_axis=0, tiled=True, axi...  16.7 us
    pallas_call x1, Pallas kernels, factors(): pl.pallas_call(functools.partial(factors_kernel, row, col), in_specs=[pl....  5.77 us
    pallas_call x1, Pallas kernels, gates(): pl.pallas_call(gate_kernel, grid=(rows // part,), in_specs=[block, fixed(...  3.07 us
    pallas_call x1, Pallas kernels, finish(): pl.pallas_call(finish_kernel, in_specs=[whole] * 5, out_specs=pl.BlockSpe...  2.38 us
  transfers between devices with their start and end apart: 2, of which 2 were waited for; matrix products, arithmetic and copies ran while one was open for 0% of the time, Pallas kernels for 3%

profile of v5, /device:TPU:8, one launch (start us, length us, event | category | flops | bytes accessed | tf_op | source)
XLA Modules:
  0.0 112.1 jit_solution(15115346407663795007)
XLA Ops:
  0.0 5.8 %factors.1 = bf16[128,2,32,128]{3,2,1,0:T(8,128)(2,1)} custom-call(s32[1024]{0:T(1024)} %mask_ref.1, s32[8,128]{1,0:T(8,128)} %bitcast.19, bf16[128,32,128]{2,1,0:T(8,128)(2,1)} %x_ref, f32[1,128]{1,0:T(1,128)} %bitcast.12, f32[1,128]{1,0:T(1,128)} %bitcast.14, bf16[4,128,128]{2,1,0:T(8,128)(2,1)} %w_hbm.1), custom_call_target="tpu_custom_call" | custom-call | tf_op jit(solution)/shard_map/factors/pallas_call | solution.py:133
  5.8 0.0 copy-start.2
  5.8 0.0 copy-start.3
  5.8 0.0 copy-start.5
  5.8 0.0 copy-start.6
  5.8 16.7 %all-to-all-start = ((bf16[128,64,128]{2,1,0:T(8,128)(2,1)}), bf16[128,64,128]{2,1,0:T(8,128)(2,1)S(1)}, u32[]{:S(2)}, u32[]{:S(2)}) async-start(bf16[128,64,128]{2,1,0:T(8,128)(2,1)} %bitcast.18), calls=%async_computation | async-start | bytes 4194304 | tf_op jit(solution)/shard_map/all_to_all | solution.py:315
  22.5 0.0 copy-done.2
  22.5 0.0 copy-done.3
  22.6 0.0 copy-done.5
  22.6 0.0 copy-done.6
  22.6 3.1 %gates.1.gate_ref = f32[128,32,128]{2,1,0:T(8,128)S(1)} custom-call(bf16[128,32,128]{2,1,0:T(8,128)(2,1)S(1)} %copy-done.2, f32[1,128]{1,0:T(1,128)S(1)} %bitcast.13, f32[1,128]{1,0:T(1,128)S(1)} %bitcast.15, bf16[128,128]{1,0:T(8,128)(2,1)S(1)} %copy-done.3), custom_call_target="tpu_custom_call" | custom-call | flops 134217728 | bytes 3145728 | tf_op jit(solution)/shard_map/gates/pallas_call | solution.py:170
  25.7 0.0 copy-start
  25.7 1.3 %copy-done = f32[128,32,128]{2,1,0:T(8,128)} copy-done((f32[128,32,128]{2,1,0:T(8,128)}, f32[128,32,128]{2,1,0:T(8,128)S(1)}, u32[]{:S(2)}) %copy-start) | copy-done | bytes 2097176
  27.0 41.6 %all-to-all-done = bf16[128,64,128]{2,1,0:T(8,128)(2,1)S(1)} async-done(((bf16[128,64,128]{2,1,0:T(8,128)(2,1)}), bf16[128,64,128]{2,1,0:T(8,128)(2,1)S(1)}, u32[]{:S(2)}, u32[]{:S(2)}) %all-to-all-start) | async-done | bytes 2097184 | tf_op jit(solution)/shard_map/all_to_all | solution.py:315
  68.6 0.1 slice_bitcast_fusion
  68.7 0.1 collective-permute-start
  68.8 0.7 half.1.half_ref
  69.5 1.9 %collective-permute-done.right_ref = bf16[128,32,128]{2,1,0:T(8,128)(2,1)S(1)} collective-permute-done((bf16[128,32,128]{2,1,0:T(8,128)(2,1)S(1)}, bf16[128,32,128]{2,1,0:T(8,128)(2,1)S(1)}, u32[]{:S(2)}, u32[]{:S(2)}) %collective-permute-start) | collective-permute-done | bytes 1048608 | tf_op jit(solution)/shard_map/ppermute | solution.py:338
  71.4 0.0 copy-start.4
  71.4 0.8 product.1
  72.2 0.0 copy-start.1
  72.2 0.0 copy-start.7
  72.2 0.0 copy-start.8
  72.2 37.5 %all_to_all.10.t_ref = bf16[128,32,128]{2,1,0:T(8,128)(2,1)S(1)} all-to-all(bf16[128,32,128]{2,1,0:T(8,128)(2,1)S(1)} %product.1), channel_id=1, replica_groups={{223,222,215,214,159,158,151,150,219,218,211,210,155,154,147,146,221,22..., dimensions={0} | all-to-all | bytes 2097152 | tf_op jit(solution)/shard_map/all_to_all | solution.py:315
  109.7 0.0 copy-done.4
  109.7 0.0 copy-done.1
  109.7 0.0 copy-done.7
  109.8 0.0 copy-done.8
  109.8 2.4 %finish.1 = bf16[128,32,128]{2,1,0:T(8,128)(2,1)} custom-call(bf16[128,32,128]{2,1,0:T(8,128)(2,1)S(1)} %all_to_all.10.t_ref, f32[128,32,128]{2,1,0:T(8,128)S(1)} %copy-done.1, f32[1,128]{1,0:T(1,128)S(1)} %bitcast.16, f32[1,128]{1,0:T(1,128)S(1)} %bitcast.17, bf16[128,128]{1,0:T(8,128)(2,1)S(1)} %copy-done.4), custom_call_target="tpu_custom_call" | custom-call | tf_op jit(solution)/shard_map/finish/pallas_call | solution.py:292
Async XLA Ops:
  5.8 16.8 %copy-start.2 = (bf16[128,32,128]{2,1,0:T(8,128)(2,1)S(1)}, bf16[128,32,128]{2,1,0:T(8,128)(2,1)}, u32[]{:S(2)}) copy-start(bf16[128,32,128]{2,1,0:T(8,128)(2,1)} %x_ref) | copy-start | bytes 3145732
  5.8 16.8 %copy-start.3 = (bf16[128,128]{1,0:T(8,128)(2,1)S(1)}, bf16[128,128]{1,0:T(8,128)(2,1)}, u32[]{:S(2)}) copy-start(bf16[128,128]{1,0:T(8,128)(2,1)} %w_ref.2) | copy-start | bytes 98308
  5.8 16.8 %copy-start.5 = (f32[128]{0:T(128)S(1)}, f32[128]{0:T(128)}, u32[]{:S(2)}) copy-start(f32[128]{0:T(128)} %param.11) | copy-start | bytes 1540
  5.8 16.7 %copy-start.6 = (f32[128]{0:T(128)S(1)}, f32[128]{0:T(128)}, u32[]{:S(2)}) copy-start(f32[128]{0:T(128)} %param.12) | copy-start | bytes 1540
  5.8 62.7 %all-to-all-start = ((bf16[128,64,128]{2,1,0:T(8,128)(2,1)}), bf16[128,64,128]{2,1,0:T(8,128)(2,1)S(1)}, u32[]{:S(2)}, u32[]{:S(2)}) async-start(bf16[128,64,128]{2,1,0:T(8,128)(2,1)} %bitcast.18), calls=%async_computation | async-start | bytes 4194304 | tf_op jit(solution)/shard_map/all_to_all | solution.py:315
  25.7 1.3 %copy-start = (f32[128,32,128]{2,1,0:T(8,128)}, f32[128,32,128]{2,1,0:T(8,128)S(1)}, u32[]{:S(2)}) copy-start(f32[128,32,128]{2,1,0:T(8,128)S(1)} %gates.1.gate_ref) | copy-start | bytes 6291460
  68.7 2.7 %collective-permute-start = (bf16[128,32,128]{2,1,0:T(8,128)(2,1)S(1)}, bf16[128,32,128]{2,1,0:T(8,128)(2,1)S(1)}, u32[]{:S(2)}, u32[]{:S(2)}) collective-permute-start(bf16[128,32,128]{2,1,0:T(8,128)(2,1)S(1)} %slice_bitcast_fusion), channel_id=1, source_target_pairs={{0,32},{32,0},{1,33},{33,1},{2,34},{34,2},{3,35},{35,3},{4,36},{36... | collective-permute-start | bytes 3145736 | tf_op jit(solution)/shard_map/ppermute | solution.py:338
  71.4 38.3 %copy-start.4 = (bf16[128,128]{1,0:T(8,128)(2,1)S(1)}, bf16[128,128]{1,0:T(8,128)(2,1)}, u32[]{:S(2)}) copy-start(bf16[128,128]{1,0:T(8,128)(2,1)} %w_ref.3) | copy-start | bytes 98308
  72.2 37.6 %copy-start.1 = (f32[128,32,128]{2,1,0:T(8,128)S(1)}, f32[128,32,128]{2,1,0:T(8,128)}, u32[]{:S(2)}) copy-start(f32[128,32,128]{2,1,0:T(8,128)} %copy-done) | copy-start | bytes 6291460
  72.2 37.5 %copy-start.7 = (f32[128]{0:T(128)S(1)}, f32[128]{0:T(128)}, u32[]{:S(2)}) copy-start(f32[128]{0:T(128)} %param.15) | copy-start | bytes 1540
  72.2 37.5 %copy-start.8 = (f32[128]{0:T(128)S(1)}, f32[128]{0:T(128)}, u32[]{:S(2)}) copy-start(f32[128]{0:T(128)} %param.16) | copy-start | bytes 1540

commit v6 on v5

--- a/solution.py
+++ b/solution.py
@@ -38,7 +38,7 @@
 
 
 def gated(gate, value):
-    return value * pltpu.reciprocal(1.0 + jnp.exp(-gate), approx=True)
+    return value / (1.0 + jnp.exp(-gate))
 
 
 def normalise(values, gain_row, bias_row):
@@ -82,16 +82,14 @@
                 [xs[pl.ds(k + d, rows, stride=APART), :].astype(jnp.bfloat16) for d in range(2)],
                 axis=0,
             )
-            projected = contract(weights, of_k, 1, 1)
-            for d in range(2):
-                mine = projected[:, d * rows : (d + 1) * rows]
-                mask = row_mask * mask_ref[first_col + n * part + k + d].astype(jnp.float32)
-                ls[pl.ds(k + d, hidden, stride=APART), :] = (
-                    gated(mine[:hidden], mine[hidden : 2 * hidden]) * mask
-                )
-                rs[pl.ds(k + d, hidden, stride=APART), :] = (
-                    gated(mine[2 * hidden : 3 * hidden], mine[3 * hidden :]) * mask
-                )
+            for side, kept in ((0, ls), (1, rs)):
+                projected = contract(weights[2 * side * hidden : 2 * (side + 1) * hidden], of_k, 1, 1)
+                for d in range(2):
+                    mine = projected[:, d * rows : (d + 1) * rows]
+                    mask = row_mask * mask_ref[first_col + n * part + k + d].astype(jnp.float32)
+                    kept[pl.ds(k + d, hidden, stride=APART), :] = (
+                        gated(mine[:hidden], mine[hidden:]) * mask
+                    )
         here = slice(n * part, (n + 1) * part)
         for h in range(hidden):
             out_ref[h, 0, here] = ls[h * APART : h * APART + part].astype(jnp.bfloat16)
@@ -139,9 +137,9 @@
             pltpu.VMEM((cols // part, rows, part, channels), jnp.bfloat16),
             pltpu.VMEM(in_weights.shape, jnp.bfloat16),
             pltpu.VMEM((hidden, 2, cols, rows), jnp.bfloat16),
-            pltpu.VMEM((rows * APART, channels), jnp.float32),
-            pltpu.VMEM((hidden * APART, rows), jnp.float32),
-            pltpu.VMEM((hidden * APART, rows), jnp.float32),
+            pltpu.VMEM(((rows + 1) * APART, channels), jnp.float32),
+            pltpu.VMEM(((hidden + 1) * APART, rows), jnp.float32),
+            pltpu.VMEM(((hidden + 1) * APART, rows), jnp.float32),
             pltpu.SemaphoreType.DMA((2 * (cols // part) + 1,)),
         ],
         compiler_params=pltpu.CompilerParams(vmem_limit_bytes=VMEM_LIMIT),
@@ -296,8 +294,8 @@
         out_shape=jax.ShapeDtypeStruct((rows, cols, channels), jnp.bfloat16),
         scratch_shapes=[
             pltpu.VMEM((rows, cols, channels), jnp.bfloat16),
-            pltpu.VMEM((hidden * APART, rows), jnp.float32),
-            pltpu.VMEM((rows * APART, channels), jnp.float32),
+            pltpu.VMEM(((hidden + 1) * APART, rows), jnp.float32),
+            pltpu.VMEM(((rows + 1) * APART, channels), jnp.float32),
             pltpu.SemaphoreType.DMA((2 * (cols // part),)),
         ],
         compiler_params=pltpu.CompilerParams(vmem_limit_bytes=32 * 1024 * 1024),

time: 113 us -> 113 us (level)
  no operation moved by 1% of the time
where the time goes in v6:
time: 113 us; the launch traced here: 112 us
  waiting for transfers between devices  43.5 us (38%)
  blocking collectives  37.5 us (33%)
  starting transfers between devices  16.8 us (15%)
  Pallas kernels  12.7 us (11%)
  local copies, waits for them, and re-layouts  1.46 us (1%)
    all_to_all x1, waiting for transfers between devices, swap(): lax.all_to_all(chunks, AXES, split_axis=0, concat_axis=0, tiled=True, axi...  41.6 us
    all_to_all x1, blocking collectives, swap(): lax.all_to_all(chunks, AXES, split_axis=0, concat_axis=0, tiled=True, axi...  37.5 us
    all_to_all x1, starting transfers between devices, swap(): lax.all_to_all(chunks, AXES, split_axis=0, concat_axis=0, tiled=True, axi...  16.7 us
    pallas_call x1, Pallas kernels, factors(): pl.pallas_call(functools.partial(factors_kernel, row, col), in_specs=[pl....  5.74 us
    pallas_call x1, Pallas kernels, gates(): pl.pallas_call(gate_kernel, grid=(rows // part,), in_specs=[block, fixed(...  3.07 us
    pallas_call x1, Pallas kernels, finish(): pl.pallas_call(finish_kernel, in_specs=[whole] * 5, out_specs=pl.BlockSpe...  2.38 us
  transfers between devices with their start and end apart: 2, of which 2 were waited for; matrix products, arithmetic and copies ran while one was open for 0% of the time, Pallas kernels for 3%

profile of v6, /device:TPU:8, one launch (start us, length us, event | category | flops | bytes accessed | tf_op | source)
XLA Modules:
  0.0 112.1 jit_solution(4303790579774930062)
XLA Ops:
  0.0 5.7 %factors.1 = bf16[128,2,32,128]{3,2,1,0:T(8,128)(2,1)} custom-call(s32[1024]{0:T(1024)} %mask_ref.1, s32[8,128]{1,0:T(8,128)} %bitcast.19, bf16[128,32,128]{2,1,0:T(8,128)(2,1)} %x_ref, f32[1,128]{1,0:T(1,128)} %bitcast.12, f32[1,128]{1,0:T(1,128)} %bitcast.14, bf16[4,128,128]{2,1,0:T(8,128)(2,1)} %w_hbm.1), custom_call_target="tpu_custom_call" | custom-call | tf_op jit(solution)/shard_map/factors/pallas_call | solution.py:131
  5.7 0.0 copy-start.2
  5.8 0.0 copy-start.3
  5.8 0.0 copy-start.5
  5.8 0.0 copy-start.6
  5.8 16.7 %all-to-all-start = ((bf16[128,64,128]{2,1,0:T(8,128)(2,1)}), bf16[128,64,128]{2,1,0:T(8,128)(2,1)S(1)}, u32[]{:S(2)}, u32[]{:S(2)}) async-start(bf16[128,64,128]{2,1,0:T(8,128)(2,1)} %bitcast.18), calls=%async_computation | async-start | bytes 4194304 | tf_op jit(solution)/shard_map/all_to_all | solution.py:313
  22.5 0.0 copy-done.2
  22.5 0.0 copy-done.3
  22.5 0.0 copy-done.5
  22.5 0.0 copy-done.6
  22.5 3.1 %gates.1.gate_ref = f32[128,32,128]{2,1,0:T(8,128)S(1)} custom-call(bf16[128,32,128]{2,1,0:T(8,128)(2,1)S(1)} %copy-done.2, f32[1,128]{1,0:T(1,128)S(1)} %bitcast.13, f32[1,128]{1,0:T(1,128)S(1)} %bitcast.15, bf16[128,128]{1,0:T(8,128)(2,1)S(1)} %copy-done.3), custom_call_target="tpu_custom_call" | custom-call | flops 134217728 | bytes 3145728 | tf_op jit(solution)/shard_map/gates/pallas_call | solution.py:168
  25.6 0.0 copy-start
  25.6 1.3 %copy-done = f32[128,32,128]{2,1,0:T(8,128)} copy-done((f32[128,32,128]{2,1,0:T(8,128)}, f32[128,32,128]{2,1,0:T(8,128)S(1)}, u32[]{:S(2)}) %copy-start) | copy-done | bytes 2097176
  26.9 41.6 %all-to-all-done = bf16[128,64,128]{2,1,0:T(8,128)(2,1)S(1)} async-done(((bf16[128,64,128]{2,1,0:T(8,128)(2,1)}), bf16[128,64,128]{2,1,0:T(8,128)(2,1)S(1)}, u32[]{:S(2)}, u32[]{:S(2)}) %all-to-all-start) | async-done | bytes 2097184 | tf_op jit(solution)/shard_map/all_to_all | solution.py:313
  68.5 0.1 slice_bitcast_fusion
  68.6 0.1 collective-permute-start
  68.7 0.7 half.1.half_ref
  69.5 1.9 %collective-permute-done.right_ref = bf16[128,32,128]{2,1,0:T(8,128)(2,1)S(1)} collective-permute-done((bf16[128,32,128]{2,1,0:T(8,128)(2,1)S(1)}, bf16[128,32,128]{2,1,0:T(8,128)(2,1)S(1)}, u32[]{:S(2)}, u32[]{:S(2)}) %collective-permute-start) | collective-permute-done | bytes 1048608 | tf_op jit(solution)/shard_map/ppermute | solution.py:336
  71.4 0.0 copy-start.4
  71.4 0.8 product.1
  72.2 0.0 copy-start.1
  72.2 0.0 copy-start.7
  72.2 0.0 copy-start.8
  72.2 37.5 %all_to_all.10.t_ref = bf16[128,32,128]{2,1,0:T(8,128)(2,1)S(1)} all-to-all(bf16[128,32,128]{2,1,0:T(8,128)(2,1)S(1)} %product.1), channel_id=1, replica_groups={{223,222,215,214,159,158,151,150,219,218,211,210,155,154,147,146,221,22..., dimensions={0} | all-to-all | bytes 2097152 | tf_op jit(solution)/shard_map/all_to_all | solution.py:313
  109.7 0.0 copy-done.4
  109.7 0.0 copy-done.1
  109.7 0.0 copy-done.7
  109.7 0.0 copy-done.8
  109.7 2.4 %finish.1 = bf16[128,32,128]{2,1,0:T(8,128)(2,1)} custom-call(bf16[128,32,128]{2,1,0:T(8,128)(2,1)S(1)} %all_to_all.10.t_ref, f32[128,32,128]{2,1,0:T(8,128)S(1)} %copy-done.1, f32[1,128]{1,0:T(1,128)S(1)} %bitcast.16, f32[1,128]{1,0:T(1,128)S(1)} %bitcast.17, bf16[128,128]{1,0:T(8,128)(2,1)S(1)} %copy-done.4), custom_call_target="tpu_custom_call" | custom-call | tf_op jit(solution)/shard_map/finish/pallas_call | solution.py:290
Async XLA Ops:
  5.7 16.7 %copy-start.2 = (bf16[128,32,128]{2,1,0:T(8,128)(2,1)S(1)}, bf16[128,32,128]{2,1,0:T(8,128)(2,1)}, u32[]{:S(2)}) copy-start(bf16[128,32,128]{2,1,0:T(8,128)(2,1)} %x_ref) | copy-start | bytes 3145732
  5.8 16.7 %copy-start.3 = (bf16[128,128]{1,0:T(8,128)(2,1)S(1)}, bf16[128,128]{1,0:T(8,128)(2,1)}, u32[]{:S(2)}) copy-start(bf16[128,128]{1,0:T(8,128)(2,1)} %w_ref.2) | copy-start | bytes 98308
  5.8 16.7 %copy-start.5 = (f32[128]{0:T(128)S(1)}, f32[128]{0:T(128)}, u32[]{:S(2)}) copy-start(f32[128]{0:T(128)} %param.11) | copy-start | bytes 1540
  5.8 16.7 %copy-start.6 = (f32[128]{0:T(128)S(1)}, f32[128]{0:T(128)}, u32[]{:S(2)}) copy-start(f32[128]{0:T(128)} %param.12) | copy-start | bytes 1540
  5.8 62.7 %all-to-all-start = ((bf16[128,64,128]{2,1,0:T(8,128)(2,1)}), bf16[128,64,128]{2,1,0:T(8,128)(2,1)S(1)}, u32[]{:S(2)}, u32[]{:S(2)}) async-start(bf16[128,64,128]{2,1,0:T(8,128)(2,1)} %bitcast.18), calls=%async_computation | async-start | bytes 4194304 | tf_op jit(solution)/shard_map/all_to_all | solution.py:313
  25.6 1.3 %copy-start = (f32[128,32,128]{2,1,0:T(8,128)}, f32[128,32,128]{2,1,0:T(8,128)S(1)}, u32[]{:S(2)}) copy-start(f32[128,32,128]{2,1,0:T(8,128)S(1)} %gates.1.gate_ref) | copy-start | bytes 6291460
  68.6 2.7 %collective-permute-start = (bf16[128,32,128]{2,1,0:T(8,128)(2,1)S(1)}, bf16[128,32,128]{2,1,0:T(8,128)(2,1)S(1)}, u32[]{:S(2)}, u32[]{:S(2)}) collective-permute-start(bf16[128,32,128]{2,1,0:T(8,128)(2,1)S(1)} %slice_bitcast_fusion), channel_id=1, source_target_pairs={{0,32},{32,0},{1,33},{33,1},{2,34},{34,2},{3,35},{35,3},{4,36},{36... | collective-permute-start | bytes 3145736 | tf_op jit(solution)/shard_map/ppermute | solution.py:336
  71.4 38.3 %copy-start.4 = (bf16[128,128]{1,0:T(8,128)(2,1)S(1)}, bf16[128,128]{1,0:T(8,128)(2,1)}, u32[]{:S(2)}) copy-start(bf16[128,128]{1,0:T(8,128)(2,1)} %w_ref.3) | copy-start | bytes 98308
  72.2 37.6 %copy-start.1 = (f32[128,32,128]{2,1,0:T(8,128)S(1)}, f32[128,32,128]{2,1,0:T(8,128)}, u32[]{:S(2)}) copy-start(f32[128,32,128]{2,1,0:T(8,128)} %copy-done) | copy-start | bytes 6291460
  72.2 37.6 %copy-start.7 = (f32[128]{0:T(128)S(1)}, f32[128]{0:T(128)}, u32[]{:S(2)}) copy-start(f32[128]{0:T(128)} %param.15) | copy-start | bytes 1540
  72.2 37.5 %copy-start.8 = (f32[128]{0:T(128)S(1)}, f32[128]{0:T(128)}, u32[]{:S(2)}) copy-start(f32[128]{0:T(128)} %param.16) | copy-start | bytes 1540

commit v7 on v6

--- a/solution.py
+++ b/solution.py
@@ -9,7 +9,7 @@
 from jax.sharding import PartitionSpec as P
 
 AXES = ("zl", "core", "x", "zh", "y")
-ORDER = ("z1", "x1", "y1", "z2", "z0", "x0", "y0")
+ORDER = ("z1", "y1", "x1", "z2", "z0", "y0", "x0")
 VMEM_LIMIT = 60 * 1024 * 1024
 APART = 17
 

time: 113 us -> 113 us (level)
  no operation moved by 1% of the time
where the time goes in v7:
time: 113 us; the launch traced here: 112 us
  waiting for transfers between devices  43.3 us (38%)
  blocking collectives  38.2 us (34%)
  starting transfers between devices  16.8 us (15%)
  Pallas kernels  12.7 us (11%)
  local copies, waits for them, and re-layouts  1.46 us (1%)
    all_to_all x1, waiting for transfers between devices, swap(): lax.all_to_all(chunks, AXES, split_axis=0, concat_axis=0, tiled=True, axi...  41.3 us
    all_to_all x1, blocking collectives, swap(): lax.all_to_all(chunks, AXES, split_axis=0, concat_axis=0, tiled=True, axi...  38.2 us
    all_to_all x1, starting transfers between devices, swap(): lax.all_to_all(chunks, AXES, split_axis=0, concat_axis=0, tiled=True, axi...  16.7 us
    pallas_call x1, Pallas kernels, factors(): pl.pallas_call(functools.partial(factors_kernel, row, col), in_specs=[pl....  5.74 us
    pallas_call x1, Pallas kernels, gates(): pl.pallas_call(gate_kernel, grid=(rows // part,), in_specs=[block, fixed(...  3.07 us
    pallas_call x1, Pallas kernels, finish(): pl.pallas_call(finish_kernel, in_specs=[whole] * 5, out_specs=pl.BlockSpe...  2.38 us
  transfers between devices with their start and end apart: 2, of which 2 were waited for; matrix products, arithmetic and copies ran while one was open for 0% of the time, Pallas kernels for 3%

profile of v7, /device:TPU:8, one launch (start us, length us, event | category | flops | bytes accessed | tf_op | source)
XLA Modules:
  0.0 112.5 jit_solution(5820369442087951062)
XLA Ops:
  0.0 5.7 %factors.1 = bf16[128,2,32,128]{3,2,1,0:T(8,128)(2,1)} custom-call(s32[1024]{0:T(1024)} %mask_ref.1, s32[8,128]{1,0:T(8,128)} %bitcast.19, bf16[128,32,128]{2,1,0:T(8,128)(2,1)} %x_ref, f32[1,128]{1,0:T(1,128)} %bitcast.12, f32[1,128]{1,0:T(1,128)} %bitcast.14, bf16[4,128,128]{2,1,0:T(8,128)(2,1)} %w_hbm.1), custom_call_target="tpu_custom_call" | custom-call | tf_op jit(solution)/shard_map/factors/pallas_call | solution.py:131
  5.7 0.0 copy-start.2
  5.8 0.0 copy-start.3
  5.8 0.0 copy-start.5
  5.8 0.0 copy-start.6
  5.8 16.7 %all-to-all-start = ((bf16[128,64,128]{2,1,0:T(8,128)(2,1)}), bf16[128,64,128]{2,1,0:T(8,128)(2,1)S(1)}, u32[]{:S(2)}, u32[]{:S(2)}) async-start(bf16[128,64,128]{2,1,0:T(8,128)(2,1)} %bitcast.18), calls=%async_computation | async-start | bytes 4194304 | tf_op jit(solution)/shard_map/all_to_all | solution.py:313
  22.5 0.0 copy-done.2
  22.5 0.0 copy-done.3
  22.5 0.0 copy-done.5
  22.5 0.0 copy-done.6
  22.5 3.1 %gates.1.gate_ref = f32[128,32,128]{2,1,0:T(8,128)S(1)} custom-call(bf16[128,32,128]{2,1,0:T(8,128)(2,1)S(1)} %copy-done.2, f32[1,128]{1,0:T(1,128)S(1)} %bitcast.13, f32[1,128]{1,0:T(1,128)S(1)} %bitcast.15, bf16[128,128]{1,0:T(8,128)(2,1)S(1)} %copy-done.3), custom_call_target="tpu_custom_call" | custom-call | flops 134217728 | bytes 3145728 | tf_op jit(solution)/shard_map/gates/pallas_call | solution.py:168
  25.6 0.0 copy-start
  25.6 1.3 %copy-done = f32[128,32,128]{2,1,0:T(8,128)} copy-done((f32[128,32,128]{2,1,0:T(8,128)}, f32[128,32,128]{2,1,0:T(8,128)S(1)}, u32[]{:S(2)}) %copy-start) | copy-done | bytes 2097176
  26.9 41.3 %all-to-all-done = bf16[128,64,128]{2,1,0:T(8,128)(2,1)S(1)} async-done(((bf16[128,64,128]{2,1,0:T(8,128)(2,1)}), bf16[128,64,128]{2,1,0:T(8,128)(2,1)S(1)}, u32[]{:S(2)}, u32[]{:S(2)}) %all-to-all-start) | async-done | bytes 2097184 | tf_op jit(solution)/shard_map/all_to_all | solution.py:313
  68.3 0.1 slice_bitcast_fusion
  68.4 0.1 collective-permute-start
  68.5 0.7 half.1.half_ref
  69.2 1.9 %collective-permute-done.right_ref = bf16[128,32,128]{2,1,0:T(8,128)(2,1)S(1)} collective-permute-done((bf16[128,32,128]{2,1,0:T(8,128)(2,1)S(1)}, bf16[128,32,128]{2,1,0:T(8,128)(2,1)S(1)}, u32[]{:S(2)}, u32[]{:S(2)}) %collective-permute-start) | collective-permute-done | bytes 1048608 | tf_op jit(solution)/shard_map/ppermute | solution.py:336
  71.1 0.0 copy-start.4
  71.1 0.7 product.1
  71.9 0.0 copy-start.1
  71.9 0.0 copy-start.7
  71.9 0.0 copy-start.8
  71.9 38.2 %all_to_all.10.t_ref = bf16[128,32,128]{2,1,0:T(8,128)(2,1)S(1)} all-to-all(bf16[128,32,128]{2,1,0:T(8,128)(2,1)S(1)} %product.1), channel_id=1, replica_groups={{223,215,222,214,159,151,158,150,219,211,218,210,155,147,154,146,207,19..., dimensions={0} | all-to-all | bytes 2097152 | tf_op jit(solution)/shard_map/all_to_all | solution.py:313
  110.1 0.0 copy-done.4
  110.1 0.0 copy-done.1
  110.1 0.0 copy-done.7
  110.1 0.0 copy-done.8
  110.1 2.4 %finish.1 = bf16[128,32,128]{2,1,0:T(8,128)(2,1)} custom-call(bf16[128,32,128]{2,1,0:T(8,128)(2,1)S(1)} %all_to_all.10.t_ref, f32[128,32,128]{2,1,0:T(8,128)S(1)} %copy-done.1, f32[1,128]{1,0:T(1,128)S(1)} %bitcast.16, f32[1,128]{1,0:T(1,128)S(1)} %bitcast.17, bf16[128,128]{1,0:T(8,128)(2,1)S(1)} %copy-done.4), custom_call_target="tpu_custom_call" | custom-call | tf_op jit(solution)/shard_map/finish/pallas_call | solution.py:290
Async XLA Ops:
  5.7 16.7 %copy-start.2 = (bf16[128,32,128]{2,1,0:T(8,128)(2,1)S(1)}, bf16[128,32,128]{2,1,0:T(8,128)(2,1)}, u32[]{:S(2)}) copy-start(bf16[128,32,128]{2,1,0:T(8,128)(2,1)} %x_ref) | copy-start | bytes 3145732
  5.8 16.7 %copy-start.3 = (bf16[128,128]{1,0:T(8,128)(2,1)S(1)}, bf16[128,128]{1,0:T(8,128)(2,1)}, u32[]{:S(2)}) copy-start(bf16[128,128]{1,0:T(8,128)(2,1)} %w_ref.2) | copy-start | bytes 98308
  5.8 16.7 %copy-start.5 = (f32[128]{0:T(128)S(1)}, f32[128]{0:T(128)}, u32[]{:S(2)}) copy-start(f32[128]{0:T(128)} %param.11) | copy-start | bytes 1540
  5.8 16.7 %copy-start.6 = (f32[128]{0:T(128)S(1)}, f32[128]{0:T(128)}, u32[]{:S(2)}) copy-start(f32[128]{0:T(128)} %param.12) | copy-start | bytes 1540
  5.8 62.5 %all-to-all-start = ((bf16[128,64,128]{2,1,0:T(8,128)(2,1)}), bf16[128,64,128]{2,1,0:T(8,128)(2,1)S(1)}, u32[]{:S(2)}, u32[]{:S(2)}) async-start(bf16[128,64,128]{2,1,0:T(8,128)(2,1)} %bitcast.18), calls=%async_computation | async-start | bytes 4194304 | tf_op jit(solution)/shard_map/all_to_all | solution.py:313
  25.6 1.3 %copy-start = (f32[128,32,128]{2,1,0:T(8,128)}, f32[128,32,128]{2,1,0:T(8,128)S(1)}, u32[]{:S(2)}) copy-start(f32[128,32,128]{2,1,0:T(8,128)S(1)} %gates.1.gate_ref) | copy-start | bytes 6291460
  68.4 2.7 %collective-permute-start = (bf16[128,32,128]{2,1,0:T(8,128)(2,1)S(1)}, bf16[128,32,128]{2,1,0:T(8,128)(2,1)S(1)}, u32[]{:S(2)}, u32[]{:S(2)}) collective-permute-start(bf16[128,32,128]{2,1,0:T(8,128)(2,1)S(1)} %slice_bitcast_fusion), channel_id=1, source_target_pairs={{0,32},{32,0},{1,33},{33,1},{2,34},{34,2},{3,35},{35,3},{4,36},{36... | collective-permute-start | bytes 3145736 | tf_op jit(solution)/shard_map/ppermute | solution.py:336
  71.1 38.9 %copy-start.4 = (bf16[128,128]{1,0:T(8,128)(2,1)S(1)}, bf16[128,128]{1,0:T(8,128)(2,1)}, u32[]{:S(2)}) copy-start(bf16[128,128]{1,0:T(8,128)(2,1)} %w_ref.3) | copy-start | bytes 98308
  71.9 38.2 %copy-start.1 = (f32[128,32,128]{2,1,0:T(8,128)S(1)}, f32[128,32,128]{2,1,0:T(8,128)}, u32[]{:S(2)}) copy-start(f32[128,32,128]{2,1,0:T(8,128)} %copy-done) | copy-start | bytes 6291460
  71.9 38.2 %copy-start.7 = (f32[128]{0:T(128)S(1)}, f32[128]{0:T(128)}, u32[]{:S(2)}) copy-start(f32[128]{0:T(128)} %param.15) | copy-start | bytes 1540
  71.9 38.2 %copy-start.8 = (f32[128]{0:T(128)S(1)}, f32[128]{0:T(128)}, u32[]{:S(2)}) copy-start(f32[128]{0:T(128)} %param.16) | copy-start | bytes 1540

commit v8 on v7

--- a/solution.py
+++ b/solution.py
@@ -9,7 +9,7 @@
 from jax.sharding import PartitionSpec as P
 
 AXES = ("zl", "core", "x", "zh", "y")
-ORDER = ("z1", "y1", "x1", "z2", "z0", "y0", "x0")
+ORDER = ("z0", "z1", "z2", "x0", "x1", "y0", "y1")
 VMEM_LIMIT = 60 * 1024 * 1024
 APART = 17
 

time: 113 us -> 113 us (level)
  blocking collectives: 38.2 us -> 36.9 us
    all_to_all x1, blocking collectives: 38.2 us -> 36.9 us  [swap(): lax.all_to_all(chunks, AXES, split_axis=0, concat_axis=0, tiled=True, axi...]
where the time goes in v8:
time: 113 us; the launch traced here: 112 us
  waiting for transfers between devices  43.7 us (39%)
  blocking collectives  36.9 us (33%)
  starting transfers between devices  16.8 us (15%)
  Pallas kernels  12.7 us (11%)
  local copies, waits for them, and re-layouts  1.46 us (1%)
    all_to_all x1, waiting for transfers between devices, swap(): lax.all_to_all(chunks, AXES, split_axis=0, concat_axis=0, tiled=True, axi...  41.7 us
    all_to_all x1, blocking collectives, swap(): lax.all_to_all(chunks, AXES, split_axis=0, concat_axis=0, tiled=True, axi...  36.9 us
    all_to_all x1, starting transfers between devices, swap(): lax.all_to_all(chunks, AXES, split_axis=0, concat_axis=0, tiled=True, axi...  16.7 us
    pallas_call x1, Pallas kernels, factors(): pl.pallas_call(functools.partial(factors_kernel, row, col), in_specs=[pl....  5.74 us
    pallas_call x1, Pallas kernels, gates(): pl.pallas_call(gate_kernel, grid=(rows // part,), in_specs=[block, fixed(...  3.07 us
    pallas_call x1, Pallas kernels, finish(): pl.pallas_call(finish_kernel, in_specs=[whole] * 5, out_specs=pl.BlockSpe...  2.37 us
  transfers between devices with their start and end apart: 2, of which 2 were waited for; matrix products, arithmetic and copies ran while one was open for 0% of the time, Pallas kernels for 3%

profile of v8, /device:TPU:8, one launch (start us, length us, event | category | flops | bytes accessed | tf_op | source)
XLA Modules:
  0.0 111.6 jit_solution(4664480739022798783)
XLA Ops:
  0.0 5.7 %factors.1 = bf16[128,2,32,128]{3,2,1,0:T(8,128)(2,1)} custom-call(s32[1024]{0:T(1024)} %mask_ref.1, s32[8,128]{1,0:T(8,128)} %bitcast.19, bf16[128,32,128]{2,1,0:T(8,128)(2,1)} %x_ref, f32[1,128]{1,0:T(1,128)} %bitcast.12, f32[1,128]{1,0:T(1,128)} %bitcast.14, bf16[4,128,128]{2,1,0:T(8,128)(2,1)} %w_hbm.1), custom_call_target="tpu_custom_call" | custom-call | tf_op jit(solution)/shard_map/factors/pallas_call | solution.py:131
  5.7 0.0 copy-start.2
  5.8 0.0 copy-start.3
  5.8 0.0 copy-start.5
  5.8 0.0 copy-start.6
  5.8 16.7 %all-to-all-start = ((bf16[128,64,128]{2,1,0:T(8,128)(2,1)}), bf16[128,64,128]{2,1,0:T(8,128)(2,1)S(1)}, u32[]{:S(2)}, u32[]{:S(2)}) async-start(bf16[128,64,128]{2,1,0:T(8,128)(2,1)} %bitcast.18), calls=%async_computation | async-start | bytes 4194304 | tf_op jit(solution)/shard_map/all_to_all | solution.py:313
  22.5 0.0 copy-done.2
  22.5 0.0 copy-done.3
  22.5 0.0 copy-done.5
  22.5 0.0 copy-done.6
  22.5 3.1 %gates.1.gate_ref = f32[128,32,128]{2,1,0:T(8,128)S(1)} custom-call(bf16[128,32,128]{2,1,0:T(8,128)(2,1)S(1)} %copy-done.2, f32[1,128]{1,0:T(1,128)S(1)} %bitcast.13, f32[1,128]{1,0:T(1,128)S(1)} %bitcast.15, bf16[128,128]{1,0:T(8,128)(2,1)S(1)} %copy-done.3), custom_call_target="tpu_custom_call" | custom-call | flops 134217728 | bytes 3145728 | tf_op jit(solution)/shard_map/gates/pallas_call | solution.py:168
  25.6 0.0 copy-start
  25.6 1.3 %copy-done = f32[128,32,128]{2,1,0:T(8,128)} copy-done((f32[128,32,128]{2,1,0:T(8,128)}, f32[128,32,128]{2,1,0:T(8,128)S(1)}, u32[]{:S(2)}) %copy-start) | copy-done | bytes 2097176
  26.9 41.7 %all-to-all-done = bf16[128,64,128]{2,1,0:T(8,128)(2,1)S(1)} async-done(((bf16[128,64,128]{2,1,0:T(8,128)(2,1)}), bf16[128,64,128]{2,1,0:T(8,128)(2,1)S(1)}, u32[]{:S(2)}, u32[]{:S(2)}) %all-to-all-start) | async-done | bytes 2097184 | tf_op jit(solution)/shard_map/all_to_all | solution.py:313
  68.7 0.1 slice_bitcast_fusion
  68.8 0.1 collective-permute-start
  68.9 0.7 half.1.half_ref
  69.6 1.9 %collective-permute-done.right_ref = bf16[128,32,128]{2,1,0:T(8,128)(2,1)S(1)} collective-permute-done((bf16[128,32,128]{2,1,0:T(8,128)(2,1)S(1)}, bf16[128,32,128]{2,1,0:T(8,128)(2,1)S(1)}, u32[]{:S(2)}, u32[]{:S(2)}) %collective-permute-start) | collective-permute-done | bytes 1048608 | tf_op jit(solution)/shard_map/ppermute | solution.py:336
  71.5 0.0 copy-start.4
  71.5 0.7 product.1
  72.3 0.0 copy-start.1
  72.3 0.0 copy-start.7
  72.3 0.0 copy-start.8
  72.3 36.9 %all_to_all.10.t_ref = bf16[128,32,128]{2,1,0:T(8,128)(2,1)S(1)} all-to-all(bf16[128,32,128]{2,1,0:T(8,128)(2,1)S(1)} %product.1), channel_id=1, replica_groups={{223,221,222,220,207,205,206,204,215,213,214,212,199,197,198,196,219,21..., dimensions={0} | all-to-all | bytes 2097152 | tf_op jit(solution)/shard_map/all_to_all | solution.py:313
  109.2 0.0 copy-done.4
  109.2 0.0 copy-done.1
  109.2 0.0 copy-done.7
  109.2 0.0 copy-done.8
  109.2 2.4 %finish.1 = bf16[128,32,128]{2,1,0:T(8,128)(2,1)} custom-call(bf16[128,32,128]{2,1,0:T(8,128)(2,1)S(1)} %all_to_all.10.t_ref, f32[128,32,128]{2,1,0:T(8,128)S(1)} %copy-done.1, f32[1,128]{1,0:T(1,128)S(1)} %bitcast.16, f32[1,128]{1,0:T(1,128)S(1)} %bitcast.17, bf16[128,128]{1,0:T(8,128)(2,1)S(1)} %copy-done.4), custom_call_target="tpu_custom_call" | custom-call | tf_op jit(solution)/shard_map/finish/pallas_call | solution.py:290
Async XLA Ops:
  5.7 16.7 %copy-start.2 = (bf16[128,32,128]{2,1,0:T(8,128)(2,1)S(1)}, bf16[128,32,128]{2,1,0:T(8,128)(2,1)}, u32[]{:S(2)}) copy-start(bf16[128,32,128]{2,1,0:T(8,128)(2,1)} %x_ref) | copy-start | bytes 3145732
  5.8 16.7 %copy-start.3 = (bf16[128,128]{1,0:T(8,128)(2,1)S(1)}, bf16[128,128]{1,0:T(8,128)(2,1)}, u32[]{:S(2)}) copy-start(bf16[128,128]{1,0:T(8,128)(2,1)} %w_ref.2) | copy-start | bytes 98308
  5.8 16.7 %copy-start.5 = (f32[128]{0:T(128)S(1)}, f32[128]{0:T(128)}, u32[]{:S(2)}) copy-start(f32[128]{0:T(128)} %param.11) | copy-start | bytes 1540
  5.8 16.7 %copy-start.6 = (f32[128]{0:T(128)S(1)}, f32[128]{0:T(128)}, u32[]{:S(2)}) copy-start(f32[128]{0:T(128)} %param.12) | copy-start | bytes 1540
  5.8 62.9 %all-to-all-start = ((bf16[128,64,128]{2,1,0:T(8,128)(2,1)}), bf16[128,64,128]{2,1,0:T(8,128)(2,1)S(1)}, u32[]{:S(2)}, u32[]{:S(2)}) async-start(bf16[128,64,128]{2,1,0:T(8,128)(2,1)} %bitcast.18), calls=%async_computation | async-start | bytes 4194304 | tf_op jit(solution)/shard_map/all_to_all | solution.py:313
  25.6 1.3 %copy-start = (f32[128,32,128]{2,1,0:T(8,128)}, f32[128,32,128]{2,1,0:T(8,128)S(1)}, u32[]{:S(2)}) copy-start(f32[128,32,128]{2,1,0:T(8,128)S(1)} %gates.1.gate_ref) | copy-start | bytes 6291460
  68.8 2.7 %collective-permute-start = (bf16[128,32,128]{2,1,0:T(8,128)(2,1)S(1)}, bf16[128,32,128]{2,1,0:T(8,128)(2,1)S(1)}, u32[]{:S(2)}, u32[]{:S(2)}) collective-permute-start(bf16[128,32,128]{2,1,0:T(8,128)(2,1)S(1)} %slice_bitcast_fusion), channel_id=1, source_target_pairs={{0,32},{32,0},{1,33},{33,1},{2,34},{34,2},{3,35},{35,3},{4,36},{36... | collective-permute-start | bytes 3145736 | tf_op jit(solution)/shard_map/ppermute | solution.py:336
  71.5 37.7 %copy-start.4 = (bf16[128,128]{1,0:T(8,128)(2,1)S(1)}, bf16[128,128]{1,0:T(8,128)(2,1)}, u32[]{:S(2)}) copy-start(bf16[128,128]{1,0:T(8,128)(2,1)} %w_ref.3) | copy-start | bytes 98308
  72.3 36.9 %copy-start.1 = (f32[128,32,128]{2,1,0:T(8,128)S(1)}, f32[128,32,128]{2,1,0:T(8,128)}, u32[]{:S(2)}) copy-start(f32[128,32,128]{2,1,0:T(8,128)} %copy-done) | copy-start | bytes 6291460
  72.3 36.9 %copy-start.7 = (f32[128]{0:T(128)S(1)}, f32[128]{0:T(128)}, u32[]{:S(2)}) copy-start(f32[128]{0:T(128)} %param.15) | copy-start | bytes 1540
  72.3 36.9 %copy-start.8 = (f32[128]{0:T(128)S(1)}, f32[128]{0:T(128)}, u32[]{:S(2)}) copy-start(f32[128]{0:T(128)} %param.16) | copy-start | bytes 1540
